TPU v7x, 32 devices: a whole 2x2x4 slice. The times are simulated.
32 devices in a mesh: pool: 2 (over y), grp: 4 (over x, core), shard: 4 (over z).
Axes of the slice: x: 2, y: 2, z: 4, core: 2. Of those that a mesh axis runs over, the one named last changes fastest.
Arguments:
- queries: bfloat16 [128, 6144], P(('pool', 'grp', 'shard')), may hold values from -160 to 160
- new_kv: bfloat16 [128, 2, 1024], P(('pool', 'grp', 'shard')), may hold values from -8 to 8
- suffix_kv: bfloat16 [128, 64, 2, 1024], P(('pool', 'grp', 'shard')), may hold values from -8 to 8
- suffix_len: int32 [128], P(('pool', 'grp', 'shard')), may hold values from 1 to 64, 4096 in all
- prefix_pool: bfloat16 [32, 6, 128, 2, 1024], P(('pool', 'grp', 'shard')), may hold values from -6 to 6
- prefix_table: int32 [32, 4], P(('pool', 'grp', 'shard')), may hold values from 0 to 5, as said below
- residual: bfloat16 [128, 6144], P(('pool', 'grp', 'shard')), may hold values from -6 to 6
- norm_gain: bfloat16 [6144], replicated, may hold values from 0.099609375 to 1.8984375
- expert_ids: int32 [128, 2], P(('pool', 'grp', 'shard')), may hold values from 0 to 7, as said below
- gate_weights: float32 [128, 2], P(('pool', 'grp', 'shard')), may hold values from 0.1 to 1
- expert_in: bfloat16 [8, 6144, 2, 8192], P('grp', None, None, ('pool', 'shard')), may hold values from -0.078125 to 0.078125
- expert_down: bfloat16 [8, 8192, 6144], P('grp', ('pool', 'shard')), may hold values from -0.0625 to 0.0625
Outputs:
- attended: bfloat16 [128, 6144], P(('pool', 'grp', 'shard'))
- layer_out: bfloat16 [128, 6144], P(('pool', 'grp', 'shard'))
Inputs may be any that keep to these rules, and one draw needn't show every extreme that they name: `prefix_table`: each device's 4 entries are different blocks of its pool. `expert_ids`: each row names two different experts. One expert, the same for all devices, is named by exactly 2 of the 4 rows of every device; no expert is named by more than 2 rows of one device.
All inputs are finite; a program needn't handle non-finite values. No bound on the sum of `suffix_len` on one device may be relied on, other than what follows from the above.
Results may differ from a plain program's by a relative error of at most 0.013.
Values may be sent and summed in bfloat16 or wider, within the bound.
No kernel may reach another device: no remote copies, remote signals or barrier semaphores. Data moves between devices by JAX's collectives and lax.ppermute only.
A program may use at most 192 MiB of HBM per device.

v0:
```python
import math

import jax
import jax.numpy as jnp
from jax import lax
from jax.sharding import PartitionSpec as P

QH = 48
KVH = 8
HD = 128
EXPERTS = 8
BLK = 128
SUF = 64


def attend(queries, new_kv, suffix_kv, suffix_len, pool_blocks, block_ids):
    req_count = queries.shape[0]
    groups = QH // KVH
    prefix_len = block_ids.shape[0] * BLK
    chosen = jnp.take(pool_blocks, block_ids, axis=0).reshape(prefix_len, 2, KVH, HD)
    query_heads = queries.reshape(req_count, KVH, groups, HD)
    suffix = suffix_kv.reshape(req_count, SUF, 2, KVH, HD)
    fresh = new_kv.reshape(req_count, 2, KVH, HD)
    factor = 1.0 / math.sqrt(HD)
    score_pre = (
        jnp.einsum("rkgd,tkd->rkgt", query_heads, chosen[:, 0], preferred_element_type=jnp.float32)
        * factor
    )
    score_suf = (
        jnp.einsum(
            "rkgd,rjkd->rkgj", query_heads, suffix[:, :, 0], preferred_element_type=jnp.float32
        )
        * factor
    )
    valid = (jnp.arange(SUF)[None, :] < suffix_len[:, None])[:, None, None, :]
    score_suf = jnp.where(valid, score_suf, -1e30)
    score_new = (
        jnp.einsum("rkgd,rkd->rkg", query_heads, fresh[:, 0], preferred_element_type=jnp.float32)[
            ..., None
        ]
        * factor
    )
    scores = jnp.concatenate([score_pre, score_suf, score_new], axis=-1)
    highest = jnp.max(scores, axis=-1, keepdims=True)
    weights = jnp.exp(scores - highest)
    probs = (weights / jnp.sum(weights, axis=-1, keepdims=True)).astype(jnp.bfloat16)
    result = jnp.einsum(
        "rkgt,tkd->rkgd", probs[..., :prefix_len], chosen[:, 1], preferred_element_type=jnp.float32
    )
    result = result + jnp.einsum(
        "rkgj,rjkd->rkgd",
        probs[..., prefix_len : prefix_len + SUF],
        suffix[:, :, 1],
        preferred_element_type=jnp.float32,
    )
    result = (
        result
        + probs[..., prefix_len + SUF :].astype(jnp.float32)
        * fresh[:, 1].astype(jnp.float32)[:, :, None, :]
    )
    return result.reshape(req_count, QH * HD).astype(jnp.bfloat16)


def local(
    queries,
    new_kv,
    suffix_kv,
    suffix_len,
    prefix_pool,
    prefix_table,
    residual,
    norm_gain,
    expert_ids,
    gate_weights,
    expert_in,
    expert_down,
):
    attended = attend(queries, new_kv, suffix_kv, suffix_len, prefix_pool[0], prefix_table[0])
    stream_f = (
        (residual.astype(jnp.float32) + attended.astype(jnp.float32))
        .astype(jnp.bfloat16)
        .astype(jnp.float32)
    )
    normed = (
        stream_f
        * lax.rsqrt(jnp.mean(stream_f * stream_f, axis=-1, keepdims=True) + 1e-05)
        * norm_gain.astype(jnp.float32)
    ).astype(jnp.bfloat16)
    n_pool = lax.axis_size("pool")
    n_grp = lax.axis_size("grp")
    n_shard = lax.axis_size("shard")
    local_experts = EXPERTS // n_grp
    capacity = expert_ids.shape[0] // 2
    width = normed.shape[1]
    flat_ids = expert_ids.reshape(-1)
    one_hot = (flat_ids[:, None] == jnp.arange(EXPERTS)[None, :]).astype(jnp.int32)
    rank_own = jnp.sum((jnp.cumsum(one_hot, axis=0) - one_hot) * one_hot, axis=1)
    slot_index = flat_ids * capacity + rank_own
    slot_table = slot_index[:, None] == jnp.arange(EXPERTS * capacity)[None, :]
    repeated = jnp.repeat(normed, 2, axis=0)
    buckets = jnp.einsum(
        "as,ad->sd", slot_table.astype(jnp.bfloat16), repeated, preferred_element_type=jnp.float32
    )
    buckets = buckets.astype(jnp.bfloat16).reshape(n_grp, local_experts, capacity, width)
    spread = jnp.broadcast_to(
        buckets[None, :, None], (n_pool, n_grp, n_shard, local_experts, capacity, width)
    )
    spread = spread.reshape(n_pool * n_grp * n_shard, local_experts, capacity, width)
    hidden_pre = jnp.einsum(
        "secd,edjf->secjf",
        lax.all_to_all(spread, ("pool", "grp", "shard"), split_axis=0, concat_axis=0, tiled=True),
        expert_in,
        preferred_element_type=jnp.float32,
    )
    hidden = (jax.nn.silu(hidden_pre[..., 0, :]) * hidden_pre[..., 1, :]).astype(jnp.bfloat16)
    returned = lax.all_to_all(
        jnp.einsum("secf,efd->secd", hidden, expert_down, preferred_element_type=jnp.float32),
        ("pool", "grp", "shard"),
        split_axis=0,
        concat_axis=0,
        tiled=True,
    )
    results = jnp.sum(
        returned.reshape(n_pool, n_grp, n_shard, local_experts, capacity, width), axis=(0, 2)
    )
    slot_results = results.reshape(EXPERTS * capacity, width)
    picked = jnp.dot(slot_table.astype(jnp.float32), slot_results, precision=lax.Precision.HIGHEST)
    picked = picked.reshape(-1, 2, width)
    layer_out = stream_f + gate_weights[:, 0:1] * picked[:, 0] + gate_weights[:, 1:2] * picked[:, 1]
    return (attended, layer_out.astype(jnp.bfloat16))


def solution(mesh):
    in_specs = (
        P(("pool", "grp", "shard"), None),
        P(("pool", "grp", "shard"), None, None),
        P(("pool", "grp", "shard"), None, None, None),
        P(("pool", "grp", "shard")),
        P(("pool", "grp", "shard"), None, None, None, None),
        P(("pool", "grp", "shard"), None),
        P(("pool", "grp", "shard"), None),
        P(),
        P(("pool", "grp", "shard"), None),
        P(("pool", "grp", "shard"), None),
        P("grp", None, None, ("pool", "shard")),
        P("grp", ("pool", "shard"), None),
    )
    out_specs = (P(("pool", "grp", "shard"), None), P(("pool", "grp", "shard"), None))
    return jax.shard_map(local, mesh=mesh, in_specs=in_specs, out_specs=out_specs, check_vma=False)
```

profile of v0, /device:TPU:0, one launch (start us, length us, event | category | flops | bytes accessed | tf_op | source)
XLA Modules:
  0.0 211.8 jit_solution(9799338205761690467)
XLA Ops:
  0.6 0.8 fusion.45
  1.5 0.8 compare_and_fusion
  2.3 0.7 iota_compare_fusion.4
  3.1 0.7 reshape.145
  3.8 0.9 reshape.143
  4.7 2.5 %reshape.169 = bf16[4,64,2,8,128]{4,3,2,1,0:T(8,128)(2,1)} reshape(bf16[4,64,2,1024]{3,2,1,0:T(2,128)(2,1)} %param.14) | data formatting | bytes 2097152 | tf_op jit(solution)/shard_map/reshape | solution.py:22
  7.2 2.1 slice_bitcast_fusion.6
  9.9 5.7 %gather_fusion = bf16[4,128,2,1024]{3,2,1,0:T(2,128)(2,1)} fusion(bf16[6,128,2,1024]{3,2,1,0:T(2,128)(2,1)S(1)} %bitcast.107, s32[1024]{0:T(1024)S(1)} %pad_clamp_fusion), kind=kCustom, calls=%fused_computation | custom fusion | bytes 4194320 | tf_op jit(solution)/shard_map/jit(_take)/gather | solution.py:20
  15.7 3.2 %reshape.168 = bf16[512,2,8,128]{3,2,1,0:T(8,128)(2,1)S(1)} reshape(bf16[4,128,2,1024]{3,2,1,0:T(2,128)(2,1)} %gather_fusion) | data formatting | bytes 4194304 | tf_op jit(solution)/shard_map/jit(_take)/gather | solution.py:20
  18.9 0.5 copy_select_fusion
  19.4 1.3 copy-done.2
  20.7 1.3 fusion.48
  22.4 1.5 copy.181
  25.6 1.3 fusion.16
  27.8 1.4 broadcast_in_dim.56
  29.2 43.9 %all_to_all.10 = bf16[32,2,2,6144]{3,2,1,0:T(2,128)(2,1)S(1)} all-to-all(bf16[32,2,2,6144]{3,2,1,0:T(2,128)(2,1)S(1)} %bitcast.108), channel_id=1, replica_groups=mesh['pool'=2,'grp'=4,'shard'=4] {'pool','grp','shard'}, dimensions={0} | all-to-all | bytes 3145728 | tf_op jit(solution)/shard_map/all_to_all | solution.py:111
  73.2 41.7 %fusion.8 = f32[32,2,2,2,1024]{4,0,3,2,1:T(8,128)} fusion(bf16[2,6144,2,1024,1]{3,2,1,0,4:T(2,128)(2,1)} %bitcast.111, bf16[32,2,2,6144,1]{3,2,1,0,4:T(2,128)(2,1)S(1)} %bitcast.109), kind=kOutput, calls=%fused_computation.9 | convolution fusion | flops 3221225472 | bytes 52953088 | tf_op jit(solution)/shard_map/secd,edjf->secjf/dot_general | solution.py:109
  114.8 10.8 %fusion.4 = f32[32,2,2,6144]{3,0,2,1:T(8,128)S(1)} fusion(bf16[2,1024,6144]{2,1,0:T(8,128)(2,1)} %param.23, f32[32,2,2,2,1024]{4,0,3,2,1:T(8,128)} %fusion.8), kind=kOutput, calls=%fused_computation.5 | convolution fusion | flops 1611399168 | bytes 29360128 | tf_op jit(solution)/shard_map/secf,efd->secd/dot_general | solution.py:117
  125.7 4.1 %copy.203 = f32[32,2,2,6144]{3,2,1,0:T(2,128)} copy(f32[32,2,2,6144]{3,0,2,1:T(8,128)S(1)} %fusion.4) | data formatting | bytes 6291456 | tf_op jit(solution)/shard_map/secf,efd->secd/transpose | solution.py:117
  129.8 4.2 %all-to-all-start.1 = ((f32[32,2,2,6144]{3,2,1,0:T(2,128)}), f32[32,2,2,6144]{3,2,1,0:T(2,128)}, u32[]{:S(2)}, u32[]{:S(2)}) async-start(f32[32,2,2,6144]{3,2,1,0:T(2,128)} %copy.203), calls=%async_computation.1 | async-start | bytes 6291456 | tf_op jit(solution)/shard_map/all_to_all | solution.py:116
  134.2 70.0 %all-to-all-done.1 = f32[32,2,2,6144]{3,2,1,0:T(2,128)} async-done(((f32[32,2,2,6144]{3,2,1,0:T(2,128)}), f32[32,2,2,6144]{3,2,1,0:T(2,128)}, u32[]{:S(2)}, u32[]{:S(2)}) %all-to-all-start.1) | async-done | bytes 3145760 | tf_op jit(solution)/shard_map/all_to_all | solution.py:116
  204.1 4.5 %reduce_sum.42 = f32[4,2,2,6144]{3,2,1,0:T(2,128)} reduce(f32[2,4,4,2,2,6144]{5,4,3,2,1,0:T(2,128)} %bitcast.32, f32[]{:T(128)} %constant.36.clone.1), dimensions={0,2}, to_apply=%region_6.7 | reduce | flops 688128 | bytes 3538948 | tf_op jit(solution)/shard_map/reduce_sum | solution.py:123
  208.7 1.3 reshape.167
  210.3 1.5 fusion.29
  (55 shorter events, 4.2 us)
Async XLA Ops:
  0.6 9.3 %copy-start = (bf16[1,6,128,2,1024]{4,3,2,1,0:T(2,128)(2,1)S(1)}, bf16[1,6,128,2,1024]{4,3,2,1,0:T(2,128)(2,1)}, u32[]{:S(2)}) copy-start(bf16[1,6,128,2,1024]{4,3,2,1,0:T(2,128)(2,1)} %param.16) | copy-start | bytes 9437188
  19.3 1.4 copy-start.2
  20.7 3.8 %copy-start.7 = (s32[4,2]{0,1:T(2,128)S(1)}, s32[4,2]{0,1:T(2,128)}, u32[]{:S(2)}) copy-start(s32[4,2]{0,1:T(2,128)} %param.20) | copy-start | bytes 100
  22.0 3.0 %copy-start.6 = (bf16[6144]{0:T(1024)(128)(2,1)S(1)}, bf16[6144]{0:T(1024)(128)(2,1)}, u32[]{:S(2)}) copy-start(bf16[6144]{0:T(1024)(128)(2,1)} %param.19) | copy-start | bytes 36868
  22.0 3.3 %copy-start.3 = (bf16[512,2,8,128]{3,0,2,1:T(8,128)(2,1)S(1)}, bf16[512,2,8,128]{3,0,2,1:T(8,128)(2,1)}, u32[]{:S(2)}) copy-start(bf16[512,2,8,128]{3,0,2,1:T(8,128)(2,1)} %copy-done.2) | copy-start | bytes 6291460
  24.3 2.6 %copy-start.5 = (bf16[4,6144]{1,0:T(4,128)(2,1)S(1)}, bf16[4,6144]{1,0:T(4,128)(2,1)}, u32[]{:S(2)}) copy-start(bf16[4,6144]{1,0:T(4,128)(2,1)} %param.18) | copy-start | bytes 147460
  26.9 0.7 copy-start.4
  129.8 4.4 %copy-start.8 = (f32[4,2]{0,1:T(2,128)S(1)}, f32[4,2]{0,1:T(2,128)}, u32[]{:S(2)}) copy-start(f32[4,2]{0,1:T(2,128)} %param.21) | copy-start | bytes 100
  129.8 74.3 %all-to-all-start.1 = ((f32[32,2,2,6144]{3,2,1,0:T(2,128)}), f32[32,2,2,6144]{3,2,1,0:T(2,128)}, u32[]{:S(2)}, u32[]{:S(2)}) async-start(f32[32,2,2,6144]{3,2,1,0:T(2,128)} %copy.203), calls=%async_computation.1 | async-start | bytes 6291456 | tf_op jit(solution)/shard_map/all_to_all | solution.py:116
  204.1 7.7 %copy-start.1 = (bf16[1,6,128,2,1024]{4,3,2,1,0:T(2,128)(2,1)S(1)}, bf16[1,6,128,2,1024]{4,3,2,1,0:T(2,128)(2,1)}, u32[]{:S(2)}) copy-start(bf16[1,6,128,2,1024]{4,3,2,1,0:T(2,128)(2,1)} %param.16) | copy-start | bytes 9437188
where the time goes:
time: 213 us; the launch traced here: 212 us
  waiting for transfers between devices  70 us (33%)
  matrix products  56.6 us (27%)
  blocking collectives  43.9 us (21%)
  local copies, waits for them, and re-layouts  26.3 us (12%)
  other arithmetic  10 us (5%)
  starting transfers between devices  4.19 us (2%)
    all_to_all x1, waiting for transfers between devices, local(): lax.all_to_all(jnp.einsum('secf,efd->secd', hidden, expert_down, preferre...  70 us
    all_to_all x1, blocking collectives, local(): lax.all_to_all(spread, ('pool', 'grp', 'shard'), split_axis=0, concat_axi...  43.9 us
    dot_general x1, matrix products, local(): jnp.einsum('secd,edjf->secjf', lax.all_to_all(spread, ('pool', 'grp', 'sh...  41.7 us
    dot_general x1, matrix products, local(): jnp.einsum('secf,efd->secd', hidden, expert_down, preferred_element_type=...  10.8 us
    gather x2, local copies, waits for them, and re-layouts, attend(): jnp.take(pool_blocks, block_ids, axis=0).reshape(prefix_len, 2, KVH, HD)  8.9 us
    reduce_sum x1, other arithmetic, local(): jnp.sum(returned.reshape(n_pool, n_grp, n_shard, local_experts, capacity,...  4.54 us
  transfers between devices with their start and end apart: 1, of which 1 were waited for; matrix products, arithmetic and copies ran while one was open for 0% of the time, Pallas kernels for 0%

commit v1 on v0

v1 whole, which is shorter than its diff:
```python
import functools
import math

import jax
import jax.numpy as jnp
from jax import lax
from jax.experimental import pallas as pl
from jax.experimental.pallas import tpu as pltpu
from jax.sharding import PartitionSpec as P

QH = 48
KVH = 8
HD = 128
EXPERTS = 8
BLK = 128
SUF = 64
ALL = ("pool", "grp", "shard")
F32 = jnp.float32
BF16 = jnp.bfloat16
LANES = 128
FIELDS = 5


def attend_kernel(
    table, lens, q_ref, new_ref, suf_ref, pool_ref, res_ref, gain_ref, ids_ref, gate_ref,
    att_ref, sent_ref, kv, att_f, sem,
):
    reqs, width = q_ref.shape
    groups = QH // KVH
    blocks = table.shape[1]
    pool_rows = pool_ref.shape[1] * 2 * BLK
    pre, suf = blocks * 2 * BLK, reqs * SUF * 2
    total = kv.shape[1]
    pool2 = pool_ref.reshape(pool_rows, KVH * HD)
    suf2 = suf_ref.reshape(suf, KVH * HD)

    def copies(k):
        cols = pl.ds(k * HD, HD)
        out = [
            pltpu.make_async_copy(
                pool2.at[pl.ds(table[0, b] * (2 * BLK), 2 * BLK), cols],
                kv.at[k, pl.ds(b * 2 * BLK, 2 * BLK)],
                sem.at[k, b],
            )
            for b in range(blocks)
        ]
        out.append(pltpu.make_async_copy(suf2.at[:, cols], kv.at[k, pl.ds(pre, suf)], sem.at[k, blocks]))
        return out

    for k in range(KVH):
        for c in copies(k):
            c.start()

    fresh = new_ref[...].astype(F32).reshape(2 * reqs, KVH * HD)
    fresh = jnp.concatenate([fresh, jnp.zeros((16 - 2 * reqs, KVH * HD), F32)], axis=0).astype(BF16)
    qf = q_ref[...].astype(F32)
    row = lax.broadcasted_iota(jnp.int32, (groups * reqs, total), 0)
    col = lax.broadcasted_iota(jnp.int32, (groups * reqs, total), 1)
    req = row % reqs
    own_len = jnp.zeros_like(row)
    for r in range(reqs):
        own_len = jnp.where(req == r, lens[r], own_len)
    after = col - pre
    fresh_at = after - suf
    ok_suf = (after >= 0) & (after < suf) & (after // (2 * SUF) == req) & ((after % (2 * SUF)) // 2 < own_len)
    ok_new = (fresh_at >= 0) & (fresh_at // 2 == req)
    valid = (col % 2 == 0) & ((col < pre) | ok_suf | ok_new)
    factor = 1.0 / math.sqrt(HD)

    for k in range(KVH):
        kv[k, pre + suf :, :] = jnp.zeros((total - pre - suf, HD), BF16)
        kv[k, pre + suf : pre + suf + 16, :] = fresh[:, k * HD : (k + 1) * HD]
        for c in copies(k):
            c.wait()
        q = jnp.concatenate(
            [qf[:, (k * groups + g) * HD : (k * groups + g + 1) * HD] for g in range(groups)], axis=0
        ).astype(BF16)
        pairs = kv[k]
        scores = lax.dot_general(q, pairs, (((1,), (1,)), ((), ())), preferred_element_type=F32) * factor
        scores = jnp.where(valid, scores, -1e30)
        highest = jnp.max(scores, axis=1, keepdims=True)
        weights = jnp.where(valid, jnp.exp(scores - highest), 0.0)
        probs = weights / jnp.sum(weights, axis=1, keepdims=True)
        probs = pltpu.roll(probs, 1, 1).astype(BF16)
        got = jnp.dot(probs, pairs, preferred_element_type=F32)
        for g in range(groups):
            h = k * groups + g
            att_f[:, h * HD : (h + 1) * HD] = got[g * reqs : (g + 1) * reqs]

    attended = att_f[...].astype(BF16)
    att_ref[...] = attended
    stream = (res_ref[...].astype(F32) + attended.astype(F32)).astype(BF16).astype(F32)
    mean = jnp.sum(stream * stream, axis=1, keepdims=True) * (1.0 / width)
    normed = stream * lax.rsqrt(mean + 1e-05) * gain_ref[...].astype(F32)
    sent_ref[:, :width] = normed.astype(BF16)

    lane = lax.broadcasted_iota(jnp.int32, (reqs, LANES), 1)
    expert, field = lane % EXPERTS, lane // EXPERTS
    first, second = ids_ref[:, 0:1] == expert, ids_ref[:, 1:2] == expert
    gate = jnp.where(first, gate_ref[:, 0:1], 0.0) + jnp.where(second, gate_ref[:, 1:2], 0.0)
    high = gate.astype(BF16).astype(F32)
    mid = (gate - high).astype(BF16).astype(F32)
    low = gate - high - mid
    member = (first | second).astype(F32)
    before = [jnp.zeros((1, LANES), F32)]
    for r in range(reqs - 1):
        before.append(before[-1] + member[r : r + 1])
    before = jnp.concatenate(before, axis=0)
    record = jnp.where(field == 0, high, jnp.where(field == 1, mid, jnp.where(field == 2, low, 0.0)))
    record = jnp.where((field == 3) & (before == 0.0), member, record)
    record = jnp.where((field == 4) & (before == 1.0), member, record)
    sent_ref[:, width:] = record.astype(BF16)


def attend(queries, new_kv, suffix_kv, suffix_len, pool, table, residual, gain, ids, gates):
    reqs, width = queries.shape
    total = table.shape[1] * 2 * BLK + reqs * SUF * 2 + LANES
    vmem = pl.BlockSpec(memory_space=pltpu.VMEM)
    smem = pl.BlockSpec(memory_space=pltpu.SMEM)
    hbm = pl.BlockSpec(memory_space=pl.ANY)
    return pl.pallas_call(
        attend_kernel,
        out_shape=(
            jax.ShapeDtypeStruct((reqs, width), BF16),
            jax.ShapeDtypeStruct((reqs, width + LANES), BF16),
        ),
        in_specs=[smem, smem, vmem, vmem, hbm, hbm, vmem, vmem, vmem, vmem],
        out_specs=(vmem, vmem),
        scratch_shapes=[
            pltpu.VMEM((KVH, total, HD), BF16),
            pltpu.VMEM((reqs, width), F32),
            pltpu.SemaphoreType.DMA((KVH, table.shape[1] + 1)),
        ],
        compiler_params=pltpu.CompilerParams(vmem_limit_bytes=24 * 2**20),
    )(table, suffix_len, queries, new_kv, suffix_kv, pool, residual, gain.reshape(1, width), ids, gates)


RING = 4
STEP = 768
DOWN = 512


def expert_kernel(parts, reqs, base_ref, *refs):
    x_refs = refs[:parts]
    in_ref, down_ref, near_ref, far_ref, wide, lhs, ring, down, acc, dense, ring_sem, down_sem = refs[parts:]
    experts, depth, _, units = in_ref.shape
    rows = near_ref.shape[0] * 2
    slots = rows // 2
    steps = depth // STEP
    tiles = units // LANES
    cuts = depth // DOWN
    in2 = in_ref.reshape(experts, 2 * depth, units)

    def in_copies(i):
        e, s = divmod(i, steps)
        return [
            pltpu.make_async_copy(
                in2.at[e, pl.ds(s * 2 * STEP, 2 * STEP), pl.ds(j * LANES, LANES)],
                ring.at[i % RING, j],
                ring_sem.at[i % RING, j],
            )
            for j in range(tiles)
        ]

    def down_copy(c):
        return pltpu.make_async_copy(
            down_ref.at[:, :, pl.ds(c * DOWN, DOWN)], down.at[c], down_sem.at[c]
        )

    for i in range(RING):
        for c in in_copies(i):
            c.start()

    part_rows = rows // parts
    for p in range(parts):
        wide[p * part_rows : (p + 1) * part_rows, :] = x_refs[p][...]

    base = base_ref[0]
    record = wide[:, depth:].astype(F32)
    lane = lax.broadcasted_iota(jnp.int32, record.shape, 1)
    row = lax.broadcasted_iota(jnp.int32, (rows, slots), 0)
    slot = lax.broadcasted_iota(jnp.int32, (rows, slots), 1)

    def column(field, e):
        return jnp.sum(jnp.where(lane == field * EXPERTS + e, record, 0.0), axis=1, keepdims=True)

    spread, gates = [], []
    for e in range(experts):
        first, second = column(3, base + e), column(4, base + e)
        gates.append(column(0, base + e) + column(1, base + e) + column(2, base + e))
        spread.append(
            jnp.where(row // reqs == slot // 2, jnp.where(slot % 2 == 0, first, second), 0.0)
        )
    pick = jnp.concatenate(spread, axis=1).T.astype(BF16)
    spread = [s.astype(BF16) for s in spread]
    src = lax.broadcasted_iota(jnp.int32, (LANES, 4 * LANES), 0)
    dst = lax.broadcasted_iota(jnp.int32, (LANES, 4 * LANES), 1)
    weave = (dst % (2 * LANES) == 2 * src + dst // (2 * LANES)).astype(F32).astype(BF16)

    blocks = STEP // LANES
    for s in range(steps):
        x = wide[:, s * STEP : (s + 1) * STEP]
        packed = jnp.dot(pick, x, preferred_element_type=F32).astype(BF16)
        tall = jnp.concatenate([packed[:, b * LANES : (b + 1) * LANES] for b in range(blocks)], axis=0)
        woven = jnp.dot(tall, weave, preferred_element_type=F32).astype(BF16)
        for b in range(blocks):
            at = (s * blocks + b) * 2 * LANES
            for e in range(experts):
                r0 = (b * experts + e) * slots
                lhs[e, 0:slots, at : at + 2 * LANES] = woven[r0 : r0 + slots, : 2 * LANES]
                lhs[e, slots : 2 * slots, at : at + 2 * LANES] = woven[r0 : r0 + slots, 2 * LANES :]

    for c in range(cuts):
        down_copy(c).start()

    for e in range(experts):
        for s in range(steps):
            i = e * steps + s
            for c in in_copies(i):
                c.wait()
            x = lhs[e, :, s * 2 * STEP : (s + 1) * 2 * STEP]
            for j in range(0, tiles, 2):
                w = jnp.concatenate([ring[i % RING, j], ring[i % RING, j + 1]], axis=1)
                got = jnp.dot(x, w, preferred_element_type=F32)
                cols = slice(j * LANES, (j + 2) * LANES)
                if s == 0:
                    acc[:, cols] = got
                else:
                    acc[:, cols] += got
            if i + RING < experts * steps:
                for c in in_copies(i + RING):
                    c.start()
        gate, up = acc[:slots, :], acc[slots:, :]
        hidden = (gate / (1.0 + jnp.exp(-gate)) * up).astype(BF16)
        dense[e] = jnp.dot(spread[e], hidden, preferred_element_type=F32).astype(BF16)

    for c in range(cuts):
        down_copy(c).wait()
        for j in range(0, DOWN, 2 * LANES):
            out = gates[0] * jnp.dot(dense[0], down[c, 0, :, j : j + 2 * LANES], preferred_element_type=F32)
            for e in range(1, experts):
                out += gates[e] * jnp.dot(
                    dense[e], down[c, e, :, j : j + 2 * LANES], preferred_element_type=F32
                )
            out = out.astype(BF16)
            cols = slice(c * DOWN + j, c * DOWN + j + 2 * LANES)
            near_ref[:, cols] = out[: rows // 2]
            far_ref[:, cols] = out[rows // 2 :]


def experts_of(reqs, base, xs, expert_in, expert_down):
    experts, depth, _, units = expert_in.shape
    parts = len(xs)
    rows = parts * xs[0].shape[0]
    vmem = pl.BlockSpec(memory_space=pltpu.VMEM)
    hbm = pl.BlockSpec(memory_space=pl.ANY)
    half = jax.ShapeDtypeStruct((rows // 2, depth), BF16)
    return pl.pallas_call(
        functools.partial(expert_kernel, parts, reqs),
        out_shape=(half, half),
        in_specs=[pl.BlockSpec(memory_space=pltpu.SMEM)] + [vmem] * parts + [hbm, hbm],
        out_specs=(vmem, vmem),
        scratch_shapes=[
            pltpu.VMEM((rows, depth + LANES), BF16),
            pltpu.VMEM((experts, rows, 2 * depth), BF16),
            pltpu.VMEM((RING, units // LANES, 2 * STEP, LANES), BF16),
            pltpu.VMEM((depth // DOWN, experts, units, DOWN), BF16),
            pltpu.VMEM((rows, units), F32),
            pltpu.VMEM((experts, rows, units), BF16),
            pltpu.SemaphoreType.DMA((RING, units // LANES)),
            pltpu.SemaphoreType.DMA((depth // DOWN,)),
        ],
        compiler_params=pltpu.CompilerParams(vmem_limit_bytes=60 * 2**20),
    )(base, *xs, expert_in, expert_down)


def local(
    n_pool, n_grp, n_shard,
    queries, new_kv, suffix_kv, suffix_len, prefix_pool, prefix_table, residual, norm_gain,
    expert_ids, gate_weights, expert_in, expert_down,
):
    reqs, width = queries.shape
    attended, sent = attend(
        queries, new_kv, suffix_kv, suffix_len, prefix_pool, prefix_table, residual, norm_gain,
        expert_ids, gate_weights,
    )
    n_high = n_grp // 2

    def turn(a, d):
        return lax.ppermute(a, "shard", [(i, (i + d) % n_shard) for i in range(n_shard)])

    def across(a, dp, dg):
        pairs = []
        for p in range(n_pool):
            for g in range(n_grp):
                to = (g // 2 + dg) % n_high * 2 + g % 2
                pairs.append((p * n_grp + g, (p + dp) % n_pool * n_grp + to))
        return lax.ppermute(a, ("pool", "grp"), pairs)

    def twin(a):
        return lax.ppermute(a, "grp", [(g, g ^ 1) for g in range(n_grp)])

    offsets = [(dp, dg) for dp in range(n_pool) for dg in range(n_high)][1:]
    column = jnp.concatenate([sent] + [turn(sent, d) for d in range(1, n_shard)], axis=0)
    planes = [column] + [across(column, dp, dg) for dp, dg in offsets]
    planes = planes + [twin(a) for a in planes]

    base = (lax.axis_index("grp") * expert_in.shape[0]).astype(jnp.int32).reshape(1)
    near, far = experts_of(reqs, base, planes, expert_in, expert_down)

    back = twin(far)
    pair = (near.astype(F32) + back.astype(F32)).astype(BF16)
    pair = pair.reshape(1 + len(offsets), reqs * n_shard, width)
    total = pair[0].astype(F32)
    for i, (dp, dg) in enumerate(offsets):
        total += across(pair[i + 1], -dp, -dg).astype(F32)
    total = total.astype(BF16).reshape(n_shard, reqs, width)
    stream = (residual.astype(F32) + attended.astype(F32)).astype(BF16).astype(F32)
    out = stream + total[0].astype(F32)
    for d in range(1, n_shard):
        out += turn(total[d], -d).astype(F32)
    return attended, out.astype(BF16)


def solution(mesh):
    rows = P(ALL, None)
    in_specs = (
        rows,
        P(ALL, None, None),
        P(ALL, None, None, None),
        P(ALL),
        P(ALL, None, None, None, None),
        rows,
        rows,
        P(),
        rows,
        rows,
        P("grp", None, None, ("pool", "shard")),
        P("grp", ("pool", "shard"), None),
    )
    sizes = [mesh.shape[a] for a in ALL]
    return jax.shard_map(
        functools.partial(local, *sizes),
        mesh=mesh, in_specs=in_specs, out_specs=(rows, rows), check_vma=False,
    )
```

time: 213 us -> 106 us (0.50)
  matrix products: 56.6 us -> 0 us
  Pallas kernels: 0 us -> 44.7 us
  blocking collectives: 43.9 us -> 0 us
  waiting for transfers between devices: 70 us -> 29.6 us
  local copies, waits for them, and re-layouts: 26.3 us -> 9.75 us
  starting transfers between devices: 4.19 us -> 18.1 us
  other arithmetic: 10 us -> 2.24 us
    all_to_all x1 -> x0, waiting for transfers between devices: 70 us -> none  [local(): lax.all_to_all(jnp.einsum('secf,efd->secd', hidden, expert_down, preferre...]
    dot_general x9 -> x0, matrix products: 56.6 us -> none  [the longest x1 41.7 us: local(): jnp.einsum('secd,edjf->secjf', lax.all_to_all(spread, ('pool', 'grp', 'sh...]
    pallas_call x0 -> x2, Pallas kernels: none -> 44.7 us  [the longest x1 35 us: experts_of(): pl.pallas_call(functools.partial(expert_kernel, parts, reqs), out_shape=(...]
    all_to_all x1 -> x0, blocking collectives: 43.9 us -> none  [local(): lax.all_to_all(spread, ('pool', 'grp', 'shard'), split_axis=0, concat_axi...]
    ppermute x0 -> x17, waiting for transfers between devices: none -> 29.6 us  [the longest x6 17.3 us: across(): return lax.ppermute(a, ('pool', 'grp'), pairs)]
    ppermute x0 -> x17, starting transfers between devices: none -> 18.1 us  [the longest x6 10.2 us: turn(): lax.ppermute(a, 'shard', [(i, (i + d) % n_shard) for i in range(n_shard)])]
    gather x2 -> x0, local copies, waits for them, and re-layouts: 8.9 us -> none  [attend(): jnp.take(pool_blocks, block_ids, axis=0).reshape(prefix_len, 2, KVH, HD)]
    unnamed x21 -> x36, local copies, waits for them, and re-layouts: 1.89 us -> 8.93 us
  transfers between devices with their start and end apart: 1 -> 17, of which waited for: 1 -> 15; matrix products, arithmetic and copies ran while one was open for 0% -> 0% of each run, Pallas kernels for 0% -> 0%
where the time goes in v1:
time: 106 us; the launch traced here: 105 us
  Pallas kernels  44.7 us (42%)
  waiting for transfers between devices  29.6 us (28%)
  starting transfers between devices  18.1 us (17%)
  local copies, waits for them, and re-layouts  9.75 us (9%)
  other arithmetic  2.24 us (2%)
    pallas_call x1, Pallas kernels, experts_of(): pl.pallas_call(functools.partial(expert_kernel, parts, reqs), out_shape=(...  35 us
    ppermute x6, waiting for transfers between devices, across(): return lax.ppermute(a, ('pool', 'grp'), pairs)  17.3 us
    ppermute x6, starting transfers between devices, turn(): lax.ppermute(a, 'shard', [(i, (i + d) % n_shard) for i in range(n_shard)])  10.2 us
    pallas_call x1, Pallas kernels, attend(): pl.pallas_call(attend_kernel, out_shape=(jax.ShapeDtypeStruct((reqs, widt...  9.69 us
    unnamed x36, local copies, waits for them, and re-layouts  8.93 us
    ppermute x6, waiting for transfers between devices, turn(): lax.ppermute(a, 'shard', [(i, (i + d) % n_shard) for i in range(n_shard)])  8.88 us
    ppermute x6, starting transfers between devices, across(): return lax.ppermute(a, ('pool', 'grp'), pairs)  7.11 us
    ppermute x5, waiting for transfers between devices, twin(): return lax.ppermute(a, 'grp', [(g, g ^ 1) for g in range(n_grp)])  3.45 us
  transfers between devices with their start and end apart: 17, of which 15 were waited for; matrix products, arithmetic and copies ran while one was open for 0% of the time, Pallas kernels for 0%

profile of v1, /device:TPU:0, one launch (start us, length us, event | category | flops | bytes accessed | tf_op | source)
XLA Modules:
  0.0 105.2 jit_solution(3571007447348568015)
XLA Ops:
  2.9 1.9 %copy-done = bf16[1,6,128,2,1024]{4,3,2,1,0:T(2,128)(2,1)S(1)} copy-done((bf16[1,6,128,2,1024]{4,3,2,1,0:T(2,128)(2,1)S(1)}, bf16[1,6,128,2,1024]{4,3,2,1,0:T(2,128)(2,1)}, u32[]{:S(2)}) %copy-start) | copy-done | bytes 3145752
  4.8 1.2 %copy-done.1 = bf16[4,64,2,1024]{3,2,1,0:T(2,128)(2,1)S(1)} copy-done((bf16[4,64,2,1024]{3,2,1,0:T(2,128)(2,1)S(1)}, bf16[4,64,2,1024]{3,2,1,0:T(2,128)(2,1)}, u32[]{:S(2)}) %copy-start.1) | copy-done | bytes 1048600
  9.6 9.7 %shard_map.131 = (bf16[4,6144]{1,0:T(4,128)(2,1)}, bf16[4,6272]{1,0:T(4,128)(2,1)S(1)}) custom-call(s32[1,4]{1,0:T(1,128)S(1)} %copy-done.6, s32[4]{0:T(128)S(1)} %copy-done.7, bf16[4,6144]{1,0:T(4,128)(2,1)S(1)} %copy-done.4, bf16[4,2,1024]{2,1,0:T(2,128)(2,1)S(1)} %copy-done.5, bf16[4,64,2,1024]{3,2,1,0:T(2,128)(2,1)S(1)} %copy-done.1, ...), custom_call_target="tpu_custom_call" | custom-call | tf_op jit(solution)/shard_map/pallas_call | solution.py:121
  19.3 5.1 %collective-permute-start.2 = (bf16[4,6272]{1,0:T(4,128)(2,1)S(1)}, bf16[4,6272]{1,0:T(4,128)(2,1)S(1)}, u32[]{:S(2)}, u32[]{:S(2)}) collective-permute-start(bf16[4,6272]{1,0:T(4,128)(2,1)S(1)} %get-tuple-element.7), channel_id=1, source_target_pairs={{0,3},{1,0},{2,1},{3,2},{4,7},{5,4},{6,5},{7,6},{8,11},{9,8},{10,9... | collective-permute-start | bytes 150536 | tf_op jit(solution)/shard_map/ppermute | solution.py:290
  24.4 1.0 collective-permute-start
  25.4 1.1 %collective-permute-done.2 = bf16[4,6272]{1,0:T(4,128)(2,1)S(1)} collective-permute-done((bf16[4,6272]{1,0:T(4,128)(2,1)S(1)}, bf16[4,6272]{1,0:T(4,128)(2,1)S(1)}, u32[]{:S(2)}, u32[]{:S(2)}) %collective-permute-start.2) | collective-permute-done | bytes 50208 | tf_op jit(solution)/shard_map/ppermute | solution.py:290
  26.5 2.9 %collective-permute-done.1 = bf16[4,6272]{1,0:T(4,128)(2,1)S(1)} collective-permute-done((bf16[4,6272]{1,0:T(4,128)(2,1)S(1)}, bf16[4,6272]{1,0:T(4,128)(2,1)S(1)}, u32[]{:S(2)}, u32[]{:S(2)}) %collective-permute-start.1) | collective-permute-done | bytes 50208 | tf_op jit(solution)/shard_map/ppermute | solution.py:290
  30.5 2.5 %collective-permute-start.5 = (bf16[16,6272]{1,0:T(8,128)(2,1)S(1)}, bf16[16,6272]{1,0:T(8,128)(2,1)S(1)}, u32[]{:S(2)}, u32[]{:S(2)}) collective-permute-start(bf16[16,6272]{1,0:T(8,128)(2,1)S(1)} %pad_maximum_fusion.refs_0_), channel_id=1, source_target_pairs={{0,24},{4,28},{8,16},{12,20},{16,8},{20,12},{24,0},{28,4},{1,25},{... | collective-permute-start | bytes 602120 | tf_op jit(solution)/shard_map/ppermute | solution.py:298
  34.0 5.2 %collective-permute-done.5.refs_3_ = bf16[16,6272]{1,0:T(8,128)(2,1)S(1)} collective-permute-done((bf16[16,6272]{1,0:T(8,128)(2,1)S(1)}, bf16[16,6272]{1,0:T(8,128)(2,1)S(1)}, u32[]{:S(2)}, u32[]{:S(2)}) %collective-permute-start.5) | collective-permute-done | bytes 200736 | tf_op jit(solution)/shard_map/ppermute | solution.py:298
  39.2 1.8 %collective-permute-done.4.refs_2_ = bf16[16,6272]{1,0:T(8,128)(2,1)S(1)} collective-permute-done((bf16[16,6272]{1,0:T(8,128)(2,1)S(1)}, bf16[16,6272]{1,0:T(8,128)(2,1)S(1)}, u32[]{:S(2)}, u32[]{:S(2)}) %collective-permute-start.4) | collective-permute-done | bytes 200736 | tf_op jit(solution)/shard_map/ppermute | solution.py:298
  41.6 0.9 collective-permute-done.8.refs_6_
  43.4 35.0 %shard_map.132 = (bf16[64,6144]{1,0:T(8,128)(2,1)}, bf16[64,6144]{1,0:T(8,128)(2,1)}) custom-call(s32[1]{0:T(128)} %bitcast.base_ref, bf16[16,6272]{1,0:T(8,128)(2,1)} %copy-done.8, bf16[16,6272]{1,0:T(8,128)(2,1)} %copy-done.11, bf16[16,6272]{1,0:T(8,128)(2,1)} %copy-done.10, bf16[16,6272]{1,0:T(8,128)(2,1)} %copy-done.9, bf16[16,6272]{1,0:T(8,128)(2,1)} %copy-done.12, ...), custom_call_target="tpu_custom_call" | custom-call | tf_op jit(solution)/shard_map/pallas_call | solution.py:258
  78.8 2.3 %collective-permute-done.10 = bf16[64,6144]{1,0:T(8,128)(2,1)S(1)} collective-permute-done((bf16[64,6144]{1,0:T(8,128)(2,1)}, bf16[64,6144]{1,0:T(8,128)(2,1)S(1)}, u32[]{:S(2)}, u32[]{:S(2)}) %collective-permute-start.10) | collective-permute-done | bytes 786464 | tf_op jit(solution)/shard_map/ppermute | solution.py:301
  81.1 1.3 %add_convert_fusion = bf16[64,6144]{1,0:T(8,128)(2,1)S(1)} fusion(bf16[64,6144]{1,0:T(8,128)(2,1)S(1)} %collective-permute-done.10, bf16[64,6144]{1,0:T(8,128)(2,1)} %get-tuple-element.8), kind=kLoop, calls=%fused_computation | loop fusion | flops 1572864 | bytes 2359296 | tf_op jit(solution)/shard_map/convert_element_type | solution.py:312
  82.4 1.6 %collective-permute-start.11 = (bf16[16,6144]{1,0:T(8,128)(2,1)S(1)}, bf16[16,6144]{1,0:T(8,128)(2,1)S(1)}, u32[]{:S(2)}, u32[]{:S(2)}) collective-permute-start(bf16[16,6144]{1,0:T(8,128)(2,1)S(1)} %get-tuple-element.10), channel_id=1, source_target_pairs={{0,8},{4,12},{8,0},{12,4},{16,24},{20,28},{24,16},{28,20},{1,9},{5... | collective-permute-start | bytes 589832 | tf_op jit(solution)/shard_map/ppermute | solution.py:298
  84.0 1.5 %collective-permute-start.13 = (bf16[16,6144]{1,0:T(8,128)(2,1)S(1)}, bf16[16,6144]{1,0:T(8,128)(2,1)S(1)}, u32[]{:S(2)}, u32[]{:S(2)}) collective-permute-start(bf16[16,6144]{1,0:T(8,128)(2,1)S(1)} %get-tuple-element.11), channel_id=1, source_target_pairs={{0,24},{4,28},{8,16},{12,20},{16,8},{20,12},{24,0},{28,4},{1,25},{... | collective-permute-start | bytes 589832 | tf_op jit(solution)/shard_map/ppermute | solution.py:298
  86.0 4.2 %collective-permute-done.11 = bf16[16,6144]{1,0:T(8,128)(2,1)S(1)} collective-permute-done((bf16[16,6144]{1,0:T(8,128)(2,1)S(1)}, bf16[16,6144]{1,0:T(8,128)(2,1)S(1)}, u32[]{:S(2)}, u32[]{:S(2)}) %collective-permute-start.11) | collective-permute-done | bytes 196640 | tf_op jit(solution)/shard_map/ppermute | solution.py:298
  90.2 4.6 %collective-permute-done.13 = bf16[16,6144]{1,0:T(8,128)(2,1)S(1)} collective-permute-done((bf16[16,6144]{1,0:T(8,128)(2,1)S(1)}, bf16[16,6144]{1,0:T(8,128)(2,1)S(1)}, u32[]{:S(2)}, u32[]{:S(2)}) %collective-permute-start.13) | collective-permute-done | bytes 196640 | tf_op jit(solution)/shard_map/ppermute | solution.py:298
  94.8 1.4 %collective-permute-done.12 = bf16[16,6144]{1,0:T(8,128)(2,1)S(1)} collective-permute-done((bf16[16,6144]{1,0:T(8,128)(2,1)S(1)}, bf16[16,6144]{1,0:T(8,128)(2,1)S(1)}, u32[]{:S(2)}, u32[]{:S(2)}) %collective-permute-start.12) | collective-permute-done | bytes 196640 | tf_op jit(solution)/shard_map/ppermute | solution.py:298
  96.4 1.2 %collective-permute-start.14 = (bf16[4,6144]{1,0:T(4,128)(2,1)S(1)}, bf16[4,6144]{1,0:T(4,128)(2,1)S(1)}, u32[]{:S(2)}, u32[]{:S(2)}) collective-permute-start(bf16[4,6144]{1,0:T(4,128)(2,1)S(1)} %get-tuple-element.13), channel_id=1, source_target_pairs={{0,3},{1,0},{2,1},{3,2},{4,7},{5,4},{6,5},{7,6},{8,11},{9,8},{10,9... | collective-permute-start | bytes 147464 | tf_op jit(solution)/shard_map/ppermute | solution.py:290
  97.6 0.9 collective-permute-start.16
  98.4 2.1 %collective-permute-start.15 = (bf16[4,6144]{1,0:T(4,128)(2,1)S(1)}, bf16[4,6144]{1,0:T(4,128)(2,1)S(1)}, u32[]{:S(2)}, u32[]{:S(2)}) collective-permute-start(bf16[4,6144]{1,0:T(4,128)(2,1)S(1)} %get-tuple-element.15), channel_id=1, source_target_pairs={{0,2},{1,3},{2,0},{3,1},{4,6},{5,7},{6,4},{7,5},{8,10},{9,11},{10,... | collective-permute-start | bytes 147464 | tf_op jit(solution)/shard_map/ppermute | solution.py:290
  101.2 2.3 %collective-permute-done.16 = bf16[4,6144]{1,0:T(4,128)(2,1)S(1)} collective-permute-done((bf16[4,6144]{1,0:T(4,128)(2,1)S(1)}, bf16[4,6144]{1,0:T(4,128)(2,1)S(1)}, u32[]{:S(2)}, u32[]{:S(2)}) %collective-permute-start.16) | collective-permute-done | bytes 49184 | tf_op jit(solution)/shard_map/ppermute | solution.py:290
  103.6 0.9 collective-permute-done.15
  (55 shorter events, 11.8 us)
Async XLA Ops:
  2.9 1.9 %copy-start = (bf16[1,6,128,2,1024]{4,3,2,1,0:T(2,128)(2,1)S(1)}, bf16[1,6,128,2,1024]{4,3,2,1,0:T(2,128)(2,1)}, u32[]{:S(2)}) copy-start(bf16[1,6,128,2,1024]{4,3,2,1,0:T(2,128)(2,1)} %pool_ref.1) | copy-start | bytes 9437188
  19.3 7.2 %collective-permute-start.2 = (bf16[4,6272]{1,0:T(4,128)(2,1)S(1)}, bf16[4,6272]{1,0:T(4,128)(2,1)S(1)}, u32[]{:S(2)}, u32[]{:S(2)}) collective-permute-start(bf16[4,6272]{1,0:T(4,128)(2,1)S(1)} %get-tuple-element.7), channel_id=1, source_target_pairs={{0,3},{1,0},{2,1},{3,2},{4,7},{5,4},{6,5},{7,6},{8,11},{9,8},{10,9... | collective-permute-start | bytes 150536 | tf_op jit(solution)/shard_map/ppermute | solution.py:290
  24.4 5.0 %collective-permute-start.1 = (bf16[4,6272]{1,0:T(4,128)(2,1)S(1)}, bf16[4,6272]{1,0:T(4,128)(2,1)S(1)}, u32[]{:S(2)}, u32[]{:S(2)}) collective-permute-start(bf16[4,6272]{1,0:T(4,128)(2,1)S(1)} %get-tuple-element.7), channel_id=1, source_target_pairs={{0,2},{1,3},{2,0},{3,1},{4,6},{5,7},{6,4},{7,5},{8,10},{9,11},{10,... | collective-permute-start | bytes 150536 | tf_op jit(solution)/shard_map/ppermute | solution.py:290
  24.4 5.9 %collective-permute-start = (bf16[4,6272]{1,0:T(4,128)(2,1)S(1)}, bf16[4,6272]{1,0:T(4,128)(2,1)S(1)}, u32[]{:S(2)}, u32[]{:S(2)}) collective-permute-start(bf16[4,6272]{1,0:T(4,128)(2,1)S(1)} %get-tuple-element.7), channel_id=1, source_target_pairs={{0,1},{1,2},{2,3},{3,0},{4,5},{5,6},{6,7},{7,4},{8,9},{9,10},{10,1... | collective-permute-start | bytes 150536 | tf_op jit(solution)/shard_map/ppermute | solution.py:290
  30.5 12.3 %copy-start.8 = (bf16[16,6272]{1,0:T(8,128)(2,1)}, bf16[16,6272]{1,0:T(8,128)(2,1)S(1)}, u32[]{:S(2)}) copy-start(bf16[16,6272]{1,0:T(8,128)(2,1)S(1)} %pad_maximum_fusion.refs_0_) | copy-start | bytes 602116
  30.5 8.7 %collective-permute-start.5 = (bf16[16,6272]{1,0:T(8,128)(2,1)S(1)}, bf16[16,6272]{1,0:T(8,128)(2,1)S(1)}, u32[]{:S(2)}, u32[]{:S(2)}) collective-permute-start(bf16[16,6272]{1,0:T(8,128)(2,1)S(1)} %pad_maximum_fusion.refs_0_), channel_id=1, source_target_pairs={{0,24},{4,28},{8,16},{12,20},{16,8},{20,12},{24,0},{28,4},{1,25},{... | collective-permute-start | bytes 602120 | tf_op jit(solution)/shard_map/ppermute | solution.py:298
  33.0 8.1 %collective-permute-start.4 = (bf16[16,6272]{1,0:T(8,128)(2,1)S(1)}, bf16[16,6272]{1,0:T(8,128)(2,1)S(1)}, u32[]{:S(2)}, u32[]{:S(2)}) collective-permute-start(bf16[16,6272]{1,0:T(8,128)(2,1)S(1)} %pad_maximum_fusion.refs_0_), channel_id=1, source_target_pairs={{0,16},{4,20},{8,24},{12,28},{16,0},{20,4},{24,8},{28,12},{1,17},{... | collective-permute-start | bytes 602120 | tf_op jit(solution)/shard_map/ppermute | solution.py:298
  33.5 7.6 %collective-permute-start.3 = (bf16[16,6272]{1,0:T(8,128)(2,1)S(1)}, bf16[16,6272]{1,0:T(8,128)(2,1)S(1)}, u32[]{:S(2)}, u32[]{:S(2)}) collective-permute-start(bf16[16,6272]{1,0:T(8,128)(2,1)S(1)} %pad_maximum_fusion.refs_0_), channel_id=1, source_target_pairs={{0,8},{4,12},{8,0},{12,4},{16,24},{20,28},{24,16},{28,20},{1,9},{5... | collective-permute-start | bytes 602120 | tf_op jit(solution)/shard_map/ppermute | solution.py:298
  34.0 7.5 %collective-permute-start.6 = (bf16[16,6272]{1,0:T(8,128)(2,1)S(1)}, bf16[16,6272]{1,0:T(8,128)(2,1)S(1)}, u32[]{:S(2)}, u32[]{:S(2)}) collective-permute-start(bf16[16,6272]{1,0:T(8,128)(2,1)S(1)} %pad_maximum_fusion.refs_0_), channel_id=1, source_target_pairs={{0,4},{4,0},{8,12},{12,8},{1,5},{5,1},{9,13},{13,9},{2,6},{6,2},{1... | collective-permute-start | bytes 602120 | tf_op jit(solution)/shard_map/ppermute | solution.py:301
  39.2 3.6 %copy-start.9 = (bf16[16,6272]{1,0:T(8,128)(2,1)}, bf16[16,6272]{1,0:T(8,128)(2,1)S(1)}, u32[]{:S(2)}) copy-start(bf16[16,6272]{1,0:T(8,128)(2,1)S(1)} %collective-permute-done.5.refs_3_) | copy-start | bytes 602116
  39.2 2.4 %collective-permute-start.9 = (bf16[16,6272]{1,0:T(8,128)(2,1)S(1)}, bf16[16,6272]{1,0:T(8,128)(2,1)S(1)}, u32[]{:S(2)}, u32[]{:S(2)}) collective-permute-start(bf16[16,6272]{1,0:T(8,128)(2,1)S(1)} %collective-permute-done.5.refs_3_), channel_id=1, source_target_pairs={{0,4},{4,0},{8,12},{12,8},{1,5},{5,1},{9,13},{13,9},{2,6},{6,2},{1... | collective-permute-start | bytes 602120 | tf_op jit(solution)/shard_map/ppermute | solution.py:301
  41.0 1.7 %copy-start.10 = (bf16[16,6272]{1,0:T(8,128)(2,1)}, bf16[16,6272]{1,0:T(8,128)(2,1)S(1)}, u32[]{:S(2)}) copy-start(bf16[16,6272]{1,0:T(8,128)(2,1)S(1)} %collective-permute-done.4.refs_2_) | copy-start | bytes 602116
  41.0 1.4 %collective-permute-start.8 = (bf16[16,6272]{1,0:T(8,128)(2,1)S(1)}, bf16[16,6272]{1,0:T(8,128)(2,1)S(1)}, u32[]{:S(2)}, u32[]{:S(2)}) collective-permute-start(bf16[16,6272]{1,0:T(8,128)(2,1)S(1)} %collective-permute-done.4.refs_2_), channel_id=1, source_target_pairs={{0,4},{4,0},{8,12},{12,8},{1,5},{5,1},{9,13},{13,9},{2,6},{6,2},{1... | collective-permute-start | bytes 602120 | tf_op jit(solution)/shard_map/ppermute | solution.py:301
  41.1 1.7 %copy-start.11 = (bf16[16,6272]{1,0:T(8,128)(2,1)}, bf16[16,6272]{1,0:T(8,128)(2,1)S(1)}, u32[]{:S(2)}) copy-start(bf16[16,6272]{1,0:T(8,128)(2,1)S(1)} %collective-permute-done.3.refs_1_) | copy-start | bytes 602116
  41.1 1.6 %collective-permute-start.7 = (bf16[16,6272]{1,0:T(8,128)(2,1)S(1)}, bf16[16,6272]{1,0:T(8,128)(2,1)S(1)}, u32[]{:S(2)}, u32[]{:S(2)}) collective-permute-start(bf16[16,6272]{1,0:T(8,128)(2,1)S(1)} %collective-permute-done.3.refs_1_), channel_id=1, source_target_pairs={{0,4},{4,0},{8,12},{12,8},{1,5},{5,1},{9,13},{13,9},{2,6},{6,2},{1... | collective-permute-start | bytes 602120 | tf_op jit(solution)/shard_map/ppermute | solution.py:301
  78.5 26.0 %copy-start.3 = (bf16[4,6144]{1,0:T(4,128)(2,1)S(1)}, bf16[4,6144]{1,0:T(4,128)(2,1)}, u32[]{:S(2)}) copy-start(bf16[4,6144]{1,0:T(4,128)(2,1)} %res_ref.1) | copy-start | bytes 147460
  78.5 26.0 %copy-start.16 = (bf16[4,6144]{1,0:T(4,128)(2,1)S(1)}, bf16[4,6144]{1,0:T(4,128)(2,1)}, u32[]{:S(2)}) copy-start(bf16[4,6144]{1,0:T(4,128)(2,1)} %get-tuple-element.4) | copy-start | bytes 147460
  78.5 2.6 %collective-permute-start.10 = (bf16[64,6144]{1,0:T(8,128)(2,1)}, bf16[64,6144]{1,0:T(8,128)(2,1)S(1)}, u32[]{:S(2)}, u32[]{:S(2)}) collective-permute-start(bf16[64,6144]{1,0:T(8,128)(2,1)} %get-tuple-element.9), channel_id=1, source_target_pairs={{0,4},{4,0},{8,12},{12,8},{1,5},{5,1},{9,13},{13,9},{2,6},{6,2},{1... | collective-permute-start | bytes 2359304 | tf_op jit(solution)/shard_map/ppermute | solution.py:301
  82.4 7.8 %collective-permute-start.11 = (bf16[16,6144]{1,0:T(8,128)(2,1)S(1)}, bf16[16,6144]{1,0:T(8,128)(2,1)S(1)}, u32[]{:S(2)}, u32[]{:S(2)}) collective-permute-start(bf16[16,6144]{1,0:T(8,128)(2,1)S(1)} %get-tuple-element.10), channel_id=1, source_target_pairs={{0,8},{4,12},{8,0},{12,4},{16,24},{20,28},{24,16},{28,20},{1,9},{5... | collective-permute-start | bytes 589832 | tf_op jit(solution)/shard_map/ppermute | solution.py:298
  84.0 10.8 %collective-permute-start.13 = (bf16[16,6144]{1,0:T(8,128)(2,1)S(1)}, bf16[16,6144]{1,0:T(8,128)(2,1)S(1)}, u32[]{:S(2)}, u32[]{:S(2)}) collective-permute-start(bf16[16,6144]{1,0:T(8,128)(2,1)S(1)} %get-tuple-element.11), channel_id=1, source_target_pairs={{0,24},{4,28},{8,16},{12,20},{16,8},{20,12},{24,0},{28,4},{1,25},{... | collective-permute-start | bytes 589832 | tf_op jit(solution)/shard_map/ppermute | solution.py:298
  85.5 10.7 %collective-permute-start.12 = (bf16[16,6144]{1,0:T(8,128)(2,1)S(1)}, bf16[16,6144]{1,0:T(8,128)(2,1)S(1)}, u32[]{:S(2)}, u32[]{:S(2)}) collective-permute-start(bf16[16,6144]{1,0:T(8,128)(2,1)S(1)} %get-tuple-element.12), channel_id=1, source_target_pairs={{0,16},{4,20},{8,24},{12,28},{16,0},{20,4},{24,8},{28,12},{1,17},{... | collective-permute-start | bytes 589832 | tf_op jit(solution)/shard_map/ppermute | solution.py:298
  96.4 4.9 %collective-permute-start.14 = (bf16[4,6144]{1,0:T(4,128)(2,1)S(1)}, bf16[4,6144]{1,0:T(4,128)(2,1)S(1)}, u32[]{:S(2)}, u32[]{:S(2)}) collective-permute-start(bf16[4,6144]{1,0:T(4,128)(2,1)S(1)} %get-tuple-element.13), channel_id=1, source_target_pairs={{0,3},{1,0},{2,1},{3,2},{4,7},{5,4},{6,5},{7,6},{8,11},{9,8},{10,9... | collective-permute-start | bytes 147464 | tf_op jit(solution)/shard_map/ppermute | solution.py:290
  97.6 6.0 %collective-permute-start.16 = (bf16[4,6144]{1,0:T(4,128)(2,1)S(1)}, bf16[4,6144]{1,0:T(4,128)(2,1)S(1)}, u32[]{:S(2)}, u32[]{:S(2)}) collective-permute-start(bf16[4,6144]{1,0:T(4,128)(2,1)S(1)} %get-tuple-element.14), channel_id=1, source_target_pairs={{0,1},{1,2},{2,3},{3,0},{4,5},{5,6},{6,7},{7,4},{8,9},{9,10},{10,1... | collective-permute-start | bytes 147464 | tf_op jit(solution)/shard_map/ppermute | solution.py:290
  98.4 6.0 %collective-permute-start.15 = (bf16[4,6144]{1,0:T(4,128)(2,1)S(1)}, bf16[4,6144]{1,0:T(4,128)(2,1)S(1)}, u32[]{:S(2)}, u32[]{:S(2)}) collective-permute-start(bf16[4,6144]{1,0:T(4,128)(2,1)S(1)} %get-tuple-element.15), channel_id=1, source_target_pairs={{0,2},{1,3},{2,0},{3,1},{4,6},{5,7},{6,4},{7,5},{8,10},{9,11},{10,... | collective-permute-start | bytes 147464 | tf_op jit(solution)/shard_map/ppermute | solution.py:290
  (10 other events, 8.7 us)

commit v2 on v1

v2 whole, which is shorter than its diff:
```python
import functools
import math

import jax
import jax.numpy as jnp
from jax import lax
from jax.experimental import pallas as pl
from jax.experimental.pallas import tpu as pltpu
from jax.sharding import PartitionSpec as P

QH = 48
KVH = 8
HD = 128
EXPERTS = 8
BLK = 128
SUF = 64
ALL = ("pool", "grp", "shard")
F32 = jnp.float32
BF16 = jnp.bfloat16
LANES = 128
PARTS = 2
STEP = 768
RING = 4


def three_terms(x):
    high = x.astype(BF16).astype(F32)
    mid = (x - high).astype(BF16).astype(F32)
    return high, mid, x - high - mid


def block_copies(in_hbm, part, i, dst, sem):
    experts, depth, _, units = in_hbm.shape
    e, s = divmod(i, depth // PARTS // STEP)
    start = 2 * (part * (depth // PARTS) + s * STEP)
    pairs = in_hbm.reshape(experts, 2 * depth, units)
    return [
        pltpu.make_async_copy(
            pairs.at[e, pl.ds(start, 2 * STEP), pl.ds(j * LANES, LANES)], dst.at[j], sem.at[j]
        )
        for j in range(units // LANES)
    ]


def attend_kernel(
    table_hbm, lens_hbm, ids_hbm, gates_hbm, q_hbm, new_hbm, suf_ref, pool_ref, res_hbm, gain_hbm,
    att_ref, sent_ref,
    kv, att_f, q_ref, new_ref, res_ref, gain_ref, table, lens, ids, gates, sem, small,
):
    reqs, width = q_ref.shape
    groups = QH // KVH
    heads = KVH
    blocks = table.shape[1]
    pool_rows = pool_ref.shape[1] * 2 * BLK
    pre, suf = blocks * 2 * BLK, reqs * SUF * 2
    total = kv.shape[1]
    pool2 = pool_ref.reshape(pool_rows, KVH * HD)
    suf2 = suf_ref.reshape(suf, KVH * HD)

    pairs = [
        (table_hbm, table),
        (q_hbm, q_ref),
        (new_hbm, new_ref),
        (res_hbm, res_ref),
        (gain_hbm, gain_ref),
        (lens_hbm, lens),
        (ids_hbm, ids),
        (gates_hbm, gates),
    ]
    small_copies = [pltpu.make_async_copy(src, dst, small.at[i]) for i, (src, dst) in enumerate(pairs)]
    for c in small_copies:
        c.start()
    copies = []
    for k in range(heads):
        cols = pl.ds(k * HD, HD)
        copies.append(
            pltpu.make_async_copy(suf2.at[:, cols], kv.at[k, pl.ds(pre, suf)], sem.at[k, blocks])
        )
    for c in copies:
        c.start()
    small_copies[0].wait()
    for k in range(heads):
        cols = pl.ds(k * HD, HD)
        for b in range(blocks):
            copies.append(pltpu.make_async_copy(
                pool2.at[pl.ds(table[0, b] * (2 * BLK), 2 * BLK), cols],
                kv.at[k, pl.ds(b * 2 * BLK, 2 * BLK)],
                sem.at[k, b],
            ))
            copies[-1].start()
    for c in small_copies[1:]:
        c.wait()

    row = lax.broadcasted_iota(jnp.int32, (groups * reqs, total), 0)
    col = lax.broadcasted_iota(jnp.int32, (groups * reqs, total), 1)
    req = row % reqs
    own_len = jnp.zeros_like(row)
    for r in range(reqs):
        own_len = jnp.where(req == r, lens[r], own_len)
    after = col - pre
    fresh_at = after - suf
    ok_suf = (after >= 0) & (after < suf) & (after // (2 * SUF) == req) & ((after % (2 * SUF)) // 2 < own_len)
    ok_new = (fresh_at >= 0) & (fresh_at // 2 == req)
    valid = (col % 2 == 0) & ((col < pre) | ok_suf | ok_new)
    factor = 1.0 / math.sqrt(HD)
    for k in range(heads):
        kv[k, pre + suf :, :] = jnp.zeros((total - pre - suf, HD), BF16)

    for c in copies:
        c.wait()
    fresh = new_ref[...].astype(F32).reshape(2 * reqs, KVH * HD)
    fresh = jnp.concatenate([fresh, jnp.zeros((16 - 2 * reqs, KVH * HD), F32)], axis=0).astype(BF16)
    qf = q_ref[...].astype(F32)
    scores = []
    for k in range(heads):
        at = k * HD
        kv[k, pre + suf : pre + suf + 16, :] = fresh[:, at : at + HD]
        q = jnp.concatenate(
            [qf[:, (k * groups + g) * HD : (k * groups + g + 1) * HD] for g in range(groups)], axis=0
        ).astype(BF16)
        one = lax.dot_general(q, kv[k], (((1,), (1,)), ((), ())), preferred_element_type=F32) * factor
        scores.append(jnp.where(valid, one, -1e30))
    scores = jnp.concatenate(scores, axis=0)
    weights = jnp.exp(scores - jnp.max(scores, axis=1, keepdims=True))
    probs = weights * (1.0 / jnp.sum(weights, axis=1, keepdims=True))
    probs = pltpu.roll(probs, 1, 1).astype(BF16)
    for k in range(heads):
        rows = groups * reqs
        got = jnp.dot(probs[k * rows : (k + 1) * rows], kv[k], preferred_element_type=F32)
        for g in range(groups):
            h = k * groups + g
            att_f[:, h * HD : (h + 1) * HD] = got[g * reqs : (g + 1) * reqs]

    attended = att_f[...].astype(BF16)
    att_ref[...] = attended
    stream = (res_ref[...].astype(F32) + attended.astype(F32)).astype(BF16).astype(F32)
    mean = jnp.sum(stream * stream, axis=1, keepdims=True) * (1.0 / width)
    normed = stream * lax.rsqrt(mean + 1e-05) * gain_ref[...].astype(F32).reshape(1, width)
    normed = normed.astype(BF16)
    run = width // PARTS

    lane = lax.broadcasted_iota(jnp.int32, (reqs, LANES), 1)
    expert, field = lane % EXPERTS, lane // EXPERTS
    at = lax.broadcasted_iota(jnp.int32, (reqs, LANES), 0)
    gate = jnp.zeros((reqs, LANES), F32)
    member = jnp.zeros((reqs, LANES), F32)
    for r in range(reqs):
        for i in range(2):
            named = (at == r) & (expert == ids[i, r])
            gate = jnp.where(named, gates[i, r], gate)
            member = jnp.where(named, 1.0, member)
    before = [jnp.zeros((1, LANES), F32)]
    for r in range(reqs - 1):
        before.append(before[-1] + member[r : r + 1])
    before = jnp.concatenate(before, axis=0)
    high, mid, low = three_terms(gate)
    record = jnp.where((field == 3) & (before == 0.0), member, 0.0)
    record = jnp.where((field == 4) & (before == 1.0), member, record)
    record = jnp.where(field == 0, high, jnp.where(field == 1, mid, jnp.where(field == 2, low, record)))
    sent_ref[:, :run] = normed[:, :run]
    sent_ref[:, run : run + LANES] = record.astype(BF16)
    sent_ref[:, run + LANES :] = normed[:, run:]


def attend(table, lens, ids, gates, queries, new_kv, suffix_kv, pool, residual, gain):
    reqs, width = queries.shape
    total = table.shape[1] * 2 * BLK + reqs * SUF * 2 + LANES
    return pl.pallas_call(
        attend_kernel,
        out_shape=(
            jax.ShapeDtypeStruct((reqs, width), BF16),
            jax.ShapeDtypeStruct((reqs, width + LANES), BF16),
        ),
        in_specs=[HBM] * 10,
        out_specs=(VMEM,) * 2,
        scratch_shapes=[
            pltpu.VMEM((KVH, total, HD), BF16),
            pltpu.VMEM((reqs, width), F32),
            pltpu.VMEM((reqs, width), BF16),
            pltpu.VMEM(new_kv.shape, BF16),
            pltpu.VMEM((reqs, width), BF16),
            pltpu.VMEM((width,), BF16),
            pltpu.SMEM(table.shape, jnp.int32),
            pltpu.SMEM(lens.shape, jnp.int32),
            pltpu.SMEM(ids.shape, jnp.int32),
            pltpu.SMEM(gates.shape, F32),
            pltpu.SemaphoreType.DMA((KVH, table.shape[1] + 1)),
            pltpu.SemaphoreType.DMA((8,)),
        ],
        compiler_params=pltpu.CompilerParams(vmem_limit_bytes=10 * 2**20),
        cost_estimate=pl.CostEstimate(flops=10**8, bytes_accessed=20 * 10**6, transcendentals=0),
    )(table, lens, ids, gates, queries, new_kv, suffix_kv, pool, residual, gain)


def field_sum(record, fields, e):
    lane = lax.broadcasted_iota(jnp.int32, record.shape, 1)
    hit = lane == fields[0] * EXPERTS + e
    for f in fields[1:]:
        hit = hit | (lane == f * EXPERTS + e)
    return jnp.sum(jnp.where(hit, record, 0.0), axis=1, keepdims=True)


def spreads(record, base, experts, reqs):
    rows = record.shape[0]
    slots = rows // reqs * 2
    row = lax.broadcasted_iota(jnp.int32, (rows, slots), 0)
    slot = lax.broadcasted_iota(jnp.int32, (rows, slots), 1)
    out = []
    for e in range(experts):
        first, second = field_sum(record, (3,), base + e), field_sum(record, (4,), base + e)
        both = jnp.where(slot % 2 == 0, first, second)
        out.append(jnp.where(row // reqs == slot // 2, both, 0.0))
    return out


def expert_kernel(part, n_parts, reqs, base_ref, *refs):
    x_refs = refs[:n_parts]
    last = part == PARTS - 1
    if last:
        (acc_0, record_0, down, in_hbm, near_ref, far_ref,
         wide, lhs, ring, acc_ref, dense, ring_sem) = refs[n_parts:]
    else:
        in_hbm, acc_ref, record_ref, wide, lhs, ring, ring_sem = refs[n_parts:]
    experts, depth, _, units = in_hbm.shape
    rows = wide.shape[0]
    slots = rows // reqs * 2
    width = depth // PARTS
    steps = width // STEP
    tiles = units // LANES
    from_in = {
        i: block_copies(in_hbm, part, i, ring.at[i % RING], ring_sem.at[i % RING])
        for i in range(experts * steps)
    }
    for i in range(RING):
        for c in from_in[i]:
            c.start()

    part_rows = rows // n_parts
    for p in range(n_parts):
        wide[p * part_rows : (p + 1) * part_rows, :] = x_refs[p][...]

    base = base_ref[0]
    if last:
        record = record_0[...]
    else:
        record = wide[:, width:].astype(F32)
        record_ref[...] = record
    spread = spreads(record, base, experts, reqs)
    pick = jnp.concatenate(spread, axis=1).T.astype(BF16)
    src = lax.broadcasted_iota(jnp.int32, (LANES, 4 * LANES), 0)
    dst = lax.broadcasted_iota(jnp.int32, (LANES, 4 * LANES), 1)
    weave = (dst % (2 * LANES) == 2 * src + dst // (2 * LANES)).astype(F32).astype(BF16)

    blocks = STEP // LANES
    for s in range(steps):
        x = wide[:, s * STEP : (s + 1) * STEP]
        packed = jnp.dot(pick, x, preferred_element_type=F32).astype(BF16)
        tall = jnp.concatenate([packed[:, b * LANES : (b + 1) * LANES] for b in range(blocks)], axis=0)
        woven = jnp.dot(tall, weave, preferred_element_type=F32).astype(BF16)
        for b in range(blocks):
            at = (s * blocks + b) * 2 * LANES
            for e in range(experts):
                r0 = (b * experts + e) * slots
                lhs[e, 0:slots, at : at + 2 * LANES] = woven[r0 : r0 + slots, : 2 * LANES]
                lhs[e, slots : 2 * slots, at : at + 2 * LANES] = woven[r0 : r0 + slots, 2 * LANES :]

    for e in range(experts):
        for s in range(steps):
            i = e * steps + s
            for c in from_in[i]:
                c.wait()
            block = ring.at[i % RING]
            x = lhs[e, :, s * 2 * STEP : (s + 1) * 2 * STEP]
            for j in range(0, tiles, 2):
                w = jnp.concatenate([block[j], block[j + 1]], axis=1)
                got = jnp.dot(x, w, preferred_element_type=F32)
                cols = slice(j * LANES, (j + 2) * LANES)
                if s > 0:
                    acc_ref[e, :, cols] += got
                elif last:
                    acc_ref[e, :, cols] = acc_0[e, :, cols] + got
                else:
                    acc_ref[e, :, cols] = got
            if i + RING < experts * steps:
                for c in from_in[i + RING]:
                    c.start()
    if last:
        gates = []
        for e in range(experts):
            gate, up = acc_ref[e, :slots, :], acc_ref[e, slots:, :]
            hidden = (gate / (1.0 + jnp.exp(-gate)) * up).astype(BF16)
            dense[e] = jnp.dot(spread[e].astype(BF16), hidden, preferred_element_type=F32).astype(BF16)
            gates.append(field_sum(record, (0, 1, 2), base + e))
        for j in range(0, depth, 2 * LANES):
            cols = slice(j, j + 2 * LANES)
            out = gates[0] * jnp.dot(dense[0], down[0, :, cols], preferred_element_type=F32)
            for e in range(1, experts):
                out += gates[e] * jnp.dot(dense[e], down[e, :, cols], preferred_element_type=F32)
            out = out.astype(BF16)
            near_ref[:, cols] = out[: rows // 2]
            far_ref[:, cols] = out[rows // 2 :]


VMEM = pl.BlockSpec(memory_space=pltpu.VMEM)
SMEM = pl.BlockSpec(memory_space=pltpu.SMEM)
HBM = pl.BlockSpec(memory_space=pltpu.HBM)


def experts_of(part, reqs, base, xs, carried, expert_in):
    experts, depth, _, units = expert_in.shape
    n_parts = len(xs)
    rows = n_parts * xs[0].shape[0]
    slots = rows // reqs * 2
    width = depth // PARTS
    last = part == PARTS - 1
    half = jax.ShapeDtypeStruct((rows // 2, depth), BF16)
    acc = (experts, 2 * slots, units)
    blocks = experts * (width // STEP)
    record = jax.ShapeDtypeStruct((rows, LANES), F32)
    scratch = [
        pltpu.VMEM((rows, xs[0].shape[1]), BF16),
        pltpu.VMEM((experts, 2 * slots, 2 * width), BF16),
        pltpu.VMEM((RING, units // LANES, 2 * STEP, LANES), BF16),
    ]
    if last:
        out_shape = (half, half)
        operands = (base, *xs, *carried, expert_in)
        in_specs = [SMEM] + [VMEM] * (n_parts + 3) + [HBM]
        scratch += [
            pltpu.VMEM(acc, F32),
            pltpu.VMEM((experts, rows, units), BF16),
        ]
    else:
        out_shape = (jax.ShapeDtypeStruct(acc, F32), record)
        operands = (base, *xs, expert_in)
        in_specs = [SMEM] + [VMEM] * n_parts + [HBM]
    scratch.append(pltpu.SemaphoreType.DMA((RING, units // LANES)))
    return pl.pallas_call(
        functools.partial(expert_kernel, part, n_parts, reqs),
        out_shape=out_shape,
        in_specs=in_specs,
        out_specs=(VMEM,) * len(out_shape),
        scratch_shapes=scratch,
        compiler_params=pltpu.CompilerParams(vmem_limit_bytes=(22 if last else 21) * 2**20),
        cost_estimate=pl.CostEstimate(flops=10**9, bytes_accessed=100 * 10**6, transcendentals=0),
    )(*operands)


def local(
    n_pool, n_grp, n_shard,
    queries, new_kv, suffix_kv, suffix_len, prefix_pool, prefix_table, residual, norm_gain,
    expert_ids, gate_weights, expert_in, expert_down,
):
    reqs, width = queries.shape
    n_high = n_grp // 2
    flips = n_shard & (n_shard - 1) == 0

    def turn(a, d):
        pairs = [(i, i ^ abs(d) if flips else (i + d) % n_shard) for i in range(n_shard)]
        return lax.ppermute(a, "shard", pairs)

    def across(a, dp, dg):
        pairs = []
        for p in range(n_pool):
            for g in range(n_grp):
                to = (g // 2 + dg) % n_high * 2 + g % 2
                pairs.append((p * n_grp + g, (p + dp) % n_pool * n_grp + to))
        return lax.ppermute(a, ("pool", "grp"), pairs)

    def twin(a):
        return lax.ppermute(a, "grp", [(g, g ^ 1) for g in range(n_grp)])

    offsets = [(dp, dg) for dp in range(n_pool) for dg in range(n_high)][1:]
    base = (lax.axis_index("grp") * expert_in.shape[0]).astype(jnp.int32).reshape(1)

    def in_vmem(array):
        return pltpu.with_memory_space_constraint(array, pltpu.VMEM)

    def in_hbm(*arrays):
        return tuple(pltpu.with_memory_space_constraint(a, pltpu.HBM) for a in arrays)

    attended, sent = attend(
        *in_hbm(
            prefix_table, suffix_len, expert_ids.T, gate_weights.T, queries, new_kv, suffix_kv,
            prefix_pool, residual, norm_gain,
        )
    )
    (expert_in,) = in_hbm(expert_in)
    column = [sent] + [turn(sent, d) for d in range(1, n_shard)]
    cut = width // PARTS + LANES
    columns = [jnp.concatenate(c, axis=0) for c in ([a[:, :cut] for a in column], [a[:, cut:] for a in column])]
    def aside(a):
        return [a] + [across(a, dp, dg) for dp, dg in offsets]

    rows_0 = aside(columns[0])
    rows_0 += [twin(a) for a in rows_0]
    acc, record = experts_of(0, reqs, base, rows_0, (), expert_in)
    rows_1 = aside(columns[1])
    acc, *rows_1 = lax.optimization_barrier((acc, *rows_1))
    rows_1 += [twin(a) for a in rows_1]
    near, far = experts_of(1, reqs, base, rows_1, (acc, record, in_vmem(expert_down)), expert_in)
    pair = (near.astype(F32) + twin(far).astype(F32)).astype(BF16)

    def home_along(a, total):
        a = a.reshape(n_shard, -1, a.shape[1])
        total = total + a[0].astype(F32)
        for d in range(1, n_shard):
            total += turn(a[d], -d).astype(F32)
        return total

    def home_aside(a, total):
        a = a.reshape(1 + len(offsets), -1, a.shape[1])
        total = total + a[0].astype(F32)
        for i, (dp, dg) in enumerate(offsets):
            total += across(a[i + 1], -dp, -dg).astype(F32)
        return total

    stream = (residual.astype(F32) + attended.astype(F32)).astype(BF16).astype(F32)
    out = home_along(home_aside(pair, 0.0).astype(BF16), stream)
    return attended, out.astype(BF16)


def solution(mesh):
    rows = P(ALL, None)
    in_specs = (
        rows,
        P(ALL, None, None),
        P(ALL, None, None, None),
        P(ALL),
        P(ALL, None, None, None, None),
        rows,
        rows,
        P(),
        rows,
        rows,
        P("grp", None, None, ("pool", "shard")),
        P("grp", ("pool", "shard"), None),
    )
    sizes = [mesh.shape[a] for a in ALL]
    return jax.shard_map(
        functools.partial(local, *sizes),
        mesh=mesh, in_specs=in_specs, out_specs=(rows, rows), check_vma=False,
    )
```

time: 106 us -> 83.3 us (0.79)
  Pallas kernels: 44.7 us -> 30.9 us
  local copies, waits for them, and re-layouts: 9.75 us -> 2.46 us
  starting transfers between devices: 18.1 us -> 21.4 us
  waiting for transfers between devices: 29.6 us -> 26.4 us
  other arithmetic: 2.24 us -> 1.13 us
    pallas_call x1 -> x2, Pallas kernels: 35 us -> 25.8 us  [experts_of(): pl.pallas_call(functools.partial(expert_kernel, part, n_parts, reqs), out...]
    unnamed x36 -> x16, local copies, waits for them, and re-layouts: 8.93 us -> 2.27 us
    pallas_call x1, Pallas kernels: 9.69 us -> 5.08 us  [attend(): pl.pallas_call(attend_kernel, out_shape=(jax.ShapeDtypeStruct((reqs, widt...]
    ppermute x6 -> x9, starting transfers between devices: 7.11 us -> 10.7 us  [across(): return lax.ppermute(a, ('pool', 'grp'), pairs)]
    ppermute x6 -> x9, waiting for transfers between devices: 17.3 us -> 13.9 us  [across(): return lax.ppermute(a, ('pool', 'grp'), pairs)]
    convert_element_type x2, other arithmetic: 1.42 us -> 0.29 us  [the longest x1 0.18 us: local(): pair = (near.astype(F32) + twin(far).astype(F32)).astype(BF16)]
    ppermute x5 -> x9, waiting for transfers between devices: 3.45 us -> 3.23 us  [twin(): return lax.ppermute(a, 'grp', [(g, g ^ 1) for g in range(n_grp)])]
  transfers between devices with their start and end apart: 17 -> 24, of which waited for: 15 -> 16; matrix products, arithmetic and copies ran while one was open for 0% -> 0% of each run, Pallas kernels for 0% -> 13%
where the time goes in v2:
time: 83.3 us; the launch traced here: 83.1 us
  Pallas kernels  30.9 us (37%)
  waiting for transfers between devices  26.4 us (32%)
  starting transfers between devices  21.4 us (26%)
  local copies, waits for them, and re-layouts  2.46 us (3%)
  other arithmetic  1.13 us (1%)
  between operations  0.88 us (1%)
    pallas_call x2, Pallas kernels, experts_of(): pl.pallas_call(functools.partial(expert_kernel, part, n_parts, reqs), out...  25.8 us
    ppermute x9, waiting for transfers between devices, across(): return lax.ppermute(a, ('pool', 'grp'), pairs)  13.9 us
    ppermute x9, starting transfers between devices, across(): return lax.ppermute(a, ('pool', 'grp'), pairs)  10.7 us
    ppermute x6, starting transfers between devices, turn(): return lax.ppermute(a, 'shard', pairs)  9.31 us
    ppermute x6, waiting for transfers between devices, turn(): return lax.ppermute(a, 'shard', pairs)  9.28 us
    pallas_call x1, Pallas kernels, attend(): pl.pallas_call(attend_kernel, out_shape=(jax.ShapeDtypeStruct((reqs, widt...  5.08 us
    ppermute x9, waiting for transfers between devices, twin(): return lax.ppermute(a, 'grp', [(g, g ^ 1) for g in range(n_grp)])  3.23 us
    unnamed x16, local copies, waits for them, and re-layouts  2.27 us
  transfers between devices with their start and end apart: 24, of which 16 were waited for; matrix products, arithmetic and copies ran while one was open for 0% of the time, Pallas kernels for 13%

profile of v2, /device:TPU:0, one launch (start us, length us, event | category | flops | bytes accessed | tf_op | source)
XLA Modules:
  0.0 83.1 jit_solution(16242001246412406546)
XLA Ops:
  0.6 5.1 %shard_map.131 = (bf16[4,6144]{1,0:T(4,128)(2,1)}, bf16[4,6272]{1,0:T(4,128)(2,1)S(1)}) custom-call(s32[1,4]{1,0:T(1,128)} %table_hbm.1, s32[4]{0:T(128)} %lens_hbm.1, s32[2,4]{1,0:T(2,128)} %bitcast.5, f32[2,4]{1,0:T(2,128)} %bitcast.6, bf16[4,6144]{1,0:T(4,128)(2,1)} %q_hbm.1, bf16[4,2,1024]{2,1,0:T(2,128)(2,1)} %new_hbm.1, ...), custom_call_target="tpu_custom_call" | custom-call | flops 100000000 | bytes 20000000 | tf_op jit(solution)/shard_map/pallas_call | solution.py:168
  5.7 5.1 %collective-permute-start.2 = (bf16[4,6272]{1,0:T(4,128)(2,1)S(1)}, bf16[4,6272]{1,0:T(4,128)(2,1)S(1)}, u32[]{:S(2)}, u32[]{:S(2)}) collective-permute-start(bf16[4,6272]{1,0:T(4,128)(2,1)S(1)} %get-tuple-element.14), channel_id=1, source_target_pairs={{0,3},{1,2},{2,1},{3,0},{4,7},{5,6},{6,5},{7,4},{8,11},{9,10},{10,... | collective-permute-start | bytes 150536 | tf_op jit(solution)/shard_map/ppermute | solution.py:360
  11.5 1.6 %collective-permute-done.2 = bf16[4,6272]{1,0:T(4,128)(2,1)S(1)} collective-permute-done((bf16[4,6272]{1,0:T(4,128)(2,1)S(1)}, bf16[4,6272]{1,0:T(4,128)(2,1)S(1)}, u32[]{:S(2)}, u32[]{:S(2)}) %collective-permute-start.2) | collective-permute-done | bytes 50208 | tf_op jit(solution)/shard_map/ppermute | solution.py:360
  13.1 2.7 %collective-permute-done.1 = bf16[4,6272]{1,0:T(4,128)(2,1)S(1)} collective-permute-done((bf16[4,6272]{1,0:T(4,128)(2,1)S(1)}, bf16[4,6272]{1,0:T(4,128)(2,1)S(1)}, u32[]{:S(2)}, u32[]{:S(2)}) %collective-permute-start.1) | collective-permute-done | bytes 50208 | tf_op jit(solution)/shard_map/ppermute | solution.py:360
  16.0 2.5 %collective-permute-start.5 = (bf16[16,3200]{1,0:T(8,128)(2,1)S(1)}, bf16[16,3200]{1,0:T(8,128)(2,1)S(1)}, u32[]{:S(2)}, u32[]{:S(2)}) collective-permute-start(bf16[16,3200]{1,0:T(8,128)(2,1)S(1)} %pad_maximum_fusion.refs_0_), channel_id=1, source_target_pairs={{0,24},{4,28},{8,16},{12,20},{16,8},{20,12},{24,0},{28,4},{1,25},{... | collective-permute-start | bytes 307208 | tf_op jit(solution)/shard_map/ppermute | solution.py:368
  19.7 2.7 %collective-permute-done.5.refs_3_ = bf16[16,3200]{1,0:T(8,128)(2,1)S(1)} collective-permute-done((bf16[16,3200]{1,0:T(8,128)(2,1)S(1)}, bf16[16,3200]{1,0:T(8,128)(2,1)S(1)}, u32[]{:S(2)}, u32[]{:S(2)}) %collective-permute-start.5) | collective-permute-done | bytes 102432 | tf_op jit(solution)/shard_map/ppermute | solution.py:368
  22.3 1.0 %collective-permute-done.4.refs_2_ = bf16[16,3200]{1,0:T(8,128)(2,1)S(1)} collective-permute-done((bf16[16,3200]{1,0:T(8,128)(2,1)S(1)}, bf16[16,3200]{1,0:T(8,128)(2,1)S(1)}, u32[]{:S(2)}, u32[]{:S(2)}) %collective-permute-start.4) | collective-permute-done | bytes 102432 | tf_op jit(solution)/shard_map/ppermute | solution.py:368
  23.9 1.5 %collective-permute-start.12 = (bf16[16,3072]{1,0:T(8,128)(2,1)S(1)}, bf16[16,3072]{1,0:T(8,128)(2,1)S(1)}, u32[]{:S(2)}, u32[]{:S(2)}) collective-permute-start(bf16[16,3072]{1,0:T(8,128)(2,1)S(1)} %pad_maximum_fusion.1.refs_0_), channel_id=1, source_target_pairs={{0,24},{4,28},{8,16},{12,20},{16,8},{20,12},{24,0},{28,4},{1,25},{... | collective-permute-start | bytes 294920 | tf_op jit(solution)/shard_map/ppermute | solution.py:368
  25.4 1.2 %collective-permute-start.11 = (bf16[16,3072]{1,0:T(8,128)(2,1)S(1)}, bf16[16,3072]{1,0:T(8,128)(2,1)S(1)}, u32[]{:S(2)}, u32[]{:S(2)}) collective-permute-start(bf16[16,3072]{1,0:T(8,128)(2,1)S(1)} %pad_maximum_fusion.1.refs_0_), channel_id=1, source_target_pairs={{0,16},{4,20},{8,24},{12,28},{16,0},{20,4},{24,8},{28,12},{1,17},{... | collective-permute-start | bytes 294920 | tf_op jit(solution)/shard_map/ppermute | solution.py:368
  26.5 0.9 %collective-permute-start.10 = (bf16[16,3072]{1,0:T(8,128)(2,1)S(1)}, bf16[16,3072]{1,0:T(8,128)(2,1)S(1)}, u32[]{:S(2)}, u32[]{:S(2)}) collective-permute-start(bf16[16,3072]{1,0:T(8,128)(2,1)S(1)} %pad_maximum_fusion.1.refs_0_), channel_id=1, source_target_pairs={{0,8},{4,12},{8,0},{12,4},{16,24},{20,28},{24,16},{28,20},{1,9},{5... | collective-permute-start | bytes 294920 | tf_op jit(solution)/shard_map/ppermute | solution.py:368
  27.5 11.1 %shard_map.132 = (f32[2,128,1024]{2,1,0:T(8,128)S(1)}, f32[128,128]{1,0:T(8,128)S(1)}) custom-call(s32[1]{0:T(128)} %bitcast.2.base_ref, bf16[16,3200]{1,0:T(8,128)(2,1)S(1)} %pad_maximum_fusion.refs_0_, bf16[16,3200]{1,0:T(8,128)(2,1)S(1)} %collective-permute-done.3.refs_1_, bf16[16,3200]{1,0:T(8,128)(2,1)S(1)} %collective-permute-done.4.refs_2_, ...), custom_call_target="tpu_custom_call" | custom-call | flops 1000000000 | bytes 100000000 | tf_op jit(solution)/shard_map/pallas_call | solution.py:338
  40.7 1.0 %slice-done.4 = s8[4194304]{0:T(1024)(128)(4,1)S(1)} async-done(((s8[25165824]{0:T(1024)(128)(4,1)}), s8[4194304]{0:T(1024)(128)(4,1)S(1)}, s32[]{:S(2)}) %slice-start.4) | async-done | bytes 4194328
  41.7 1.2 %slice-done.5 = s8[4194304]{0:T(1024)(128)(4,1)S(1)} async-done(((s8[25165824]{0:T(1024)(128)(4,1)}), s8[4194304]{0:T(1024)(128)(4,1)S(1)}, s32[]{:S(2)}) %slice-start.5) | async-done | bytes 4194328
  42.9 14.7 %shard_map.133 = (bf16[64,6144]{1,0:T(8,128)(2,1)S(1)}, bf16[64,6144]{1,0:T(8,128)(2,1)S(1)}) custom-call(s32[1]{0:T(128)} %bitcast.2.base_ref, bf16[16,3072]{1,0:T(8,128)(2,1)S(1)} %pad_maximum_fusion.1.refs_0_, bf16[16,3072]{1,0:T(8,128)(2,1)S(1)} %collective-permute-done.10.refs_1_, bf16[16,3072]{1,0:T(8,128)(2,1)S(1)} %collective-permute-done.11.refs_2_, ...), custom_call_target="tpu_custom_call" | custom-call | flops 1000000000 | bytes 100000000 | tf_op jit(solution)/shard_map/pallas_call | solution.py:338
  57.8 2.3 %collective-permute-done.17 = bf16[64,6144]{1,0:T(8,128)(2,1)S(1)} collective-permute-done((bf16[64,6144]{1,0:T(8,128)(2,1)S(1)}, bf16[64,6144]{1,0:T(8,128)(2,1)S(1)}, u32[]{:S(2)}, u32[]{:S(2)}) %collective-permute-start.17) | collective-permute-done | bytes 786464 | tf_op jit(solution)/shard_map/ppermute | solution.py:371
  60.3 1.2 %collective-permute-start.18 = (bf16[16,6144]{1,0:T(8,128)(2,1)S(1)}, bf16[16,6144]{1,0:T(8,128)(2,1)S(1)}, u32[]{:S(2)}, u32[]{:S(2)}) collective-permute-start(bf16[16,6144]{1,0:T(8,128)(2,1)S(1)} %get-tuple-element.24), channel_id=1, source_target_pairs={{0,8},{4,12},{8,0},{12,4},{16,24},{20,28},{24,16},{28,20},{1,9},{5... | collective-permute-start | bytes 589832 | tf_op jit(solution)/shard_map/ppermute | solution.py:368
  61.5 1.7 %collective-permute-start.20 = (bf16[16,6144]{1,0:T(8,128)(2,1)S(1)}, bf16[16,6144]{1,0:T(8,128)(2,1)S(1)}, u32[]{:S(2)}, u32[]{:S(2)}) collective-permute-start(bf16[16,6144]{1,0:T(8,128)(2,1)S(1)} %get-tuple-element.25), channel_id=1, source_target_pairs={{0,24},{4,28},{8,16},{12,20},{16,8},{20,12},{24,0},{28,4},{1,25},{... | collective-permute-start | bytes 589832 | tf_op jit(solution)/shard_map/ppermute | solution.py:368
  63.8 4.3 %collective-permute-done.18 = bf16[16,6144]{1,0:T(8,128)(2,1)S(1)} collective-permute-done((bf16[16,6144]{1,0:T(8,128)(2,1)S(1)}, bf16[16,6144]{1,0:T(8,128)(2,1)S(1)}, u32[]{:S(2)}, u32[]{:S(2)}) %collective-permute-start.18) | collective-permute-done | bytes 196640 | tf_op jit(solution)/shard_map/ppermute | solution.py:368
  68.1 4.3 %collective-permute-done.20 = bf16[16,6144]{1,0:T(8,128)(2,1)S(1)} collective-permute-done((bf16[16,6144]{1,0:T(8,128)(2,1)S(1)}, bf16[16,6144]{1,0:T(8,128)(2,1)S(1)}, u32[]{:S(2)}, u32[]{:S(2)}) %collective-permute-start.20) | collective-permute-done | bytes 196640 | tf_op jit(solution)/shard_map/ppermute | solution.py:368
  72.4 1.4 %collective-permute-done.19 = bf16[16,6144]{1,0:T(8,128)(2,1)S(1)} collective-permute-done((bf16[16,6144]{1,0:T(8,128)(2,1)S(1)}, bf16[16,6144]{1,0:T(8,128)(2,1)S(1)}, u32[]{:S(2)}, u32[]{:S(2)}) %collective-permute-start.19) | collective-permute-done | bytes 196640 | tf_op jit(solution)/shard_map/ppermute | solution.py:368
  73.9 0.7 collective-permute-start.21
  74.7 2.8 %collective-permute-start.23 = (bf16[4,6144]{1,0:T(4,128)(2,1)S(1)}, bf16[4,6144]{1,0:T(4,128)(2,1)S(1)}, u32[]{:S(2)}, u32[]{:S(2)}) collective-permute-start(bf16[4,6144]{1,0:T(4,128)(2,1)S(1)} %get-tuple-element.28), channel_id=1, source_target_pairs={{0,3},{1,2},{2,1},{3,0},{4,7},{5,6},{6,5},{7,4},{8,11},{9,10},{10,... | collective-permute-start | bytes 147464 | tf_op jit(solution)/shard_map/ppermute | solution.py:360
  78.1 2.5 %collective-permute-done.23 = bf16[4,6144]{1,0:T(4,128)(2,1)S(1)} collective-permute-done((bf16[4,6144]{1,0:T(4,128)(2,1)S(1)}, bf16[4,6144]{1,0:T(4,128)(2,1)S(1)}, u32[]{:S(2)}, u32[]{:S(2)}) %collective-permute-start.23) | collective-permute-done | bytes 49184 | tf_op jit(solution)/shard_map/ppermute | solution.py:360
  80.5 1.9 %collective-permute-done.22 = bf16[4,6144]{1,0:T(4,128)(2,1)S(1)} collective-permute-done((bf16[4,6144]{1,0:T(4,128)(2,1)S(1)}, bf16[4,6144]{1,0:T(4,128)(2,1)S(1)}, u32[]{:S(2)}, u32[]{:S(2)}) %collective-permute-start.22) | collective-permute-done | bytes 49184 | tf_op jit(solution)/shard_map/ppermute | solution.py:360
  (59 shorter events, 7.0 us)
Async XLA Ops:
  5.7 7.4 %collective-permute-start.2 = (bf16[4,6272]{1,0:T(4,128)(2,1)S(1)}, bf16[4,6272]{1,0:T(4,128)(2,1)S(1)}, u32[]{:S(2)}, u32[]{:S(2)}) collective-permute-start(bf16[4,6272]{1,0:T(4,128)(2,1)S(1)} %get-tuple-element.14), channel_id=1, source_target_pairs={{0,3},{1,2},{2,1},{3,0},{4,7},{5,6},{6,5},{7,4},{8,11},{9,10},{10,... | collective-permute-start | bytes 150536 | tf_op jit(solution)/shard_map/ppermute | solution.py:360
  10.8 5.0 %collective-permute-start.1 = (bf16[4,6272]{1,0:T(4,128)(2,1)S(1)}, bf16[4,6272]{1,0:T(4,128)(2,1)S(1)}, u32[]{:S(2)}, u32[]{:S(2)}) collective-permute-start(bf16[4,6272]{1,0:T(4,128)(2,1)S(1)} %get-tuple-element.14), channel_id=1, source_target_pairs={{0,2},{1,3},{2,0},{3,1},{4,6},{5,7},{6,4},{7,5},{8,10},{9,11},{10,... | collective-permute-start | bytes 150536 | tf_op jit(solution)/shard_map/ppermute | solution.py:360
  10.8 5.0 %collective-permute-start = (bf16[4,6272]{1,0:T(4,128)(2,1)S(1)}, bf16[4,6272]{1,0:T(4,128)(2,1)S(1)}, u32[]{:S(2)}, u32[]{:S(2)}) collective-permute-start(bf16[4,6272]{1,0:T(4,128)(2,1)S(1)} %get-tuple-element.14), channel_id=1, source_target_pairs={{0,1},{1,0},{2,3},{3,2},{4,5},{5,4},{6,7},{7,6},{8,9},{9,8},{10,11... | collective-permute-start | bytes 150536 | tf_op jit(solution)/shard_map/ppermute | solution.py:360
  16.0 6.4 %collective-permute-start.5 = (bf16[16,3200]{1,0:T(8,128)(2,1)S(1)}, bf16[16,3200]{1,0:T(8,128)(2,1)S(1)}, u32[]{:S(2)}, u32[]{:S(2)}) collective-permute-start(bf16[16,3200]{1,0:T(8,128)(2,1)S(1)} %pad_maximum_fusion.refs_0_), channel_id=1, source_target_pairs={{0,24},{4,28},{8,16},{12,20},{16,8},{20,12},{24,0},{28,4},{1,25},{... | collective-permute-start | bytes 307208 | tf_op jit(solution)/shard_map/ppermute | solution.py:368
  18.5 4.8 %collective-permute-start.4 = (bf16[16,3200]{1,0:T(8,128)(2,1)S(1)}, bf16[16,3200]{1,0:T(8,128)(2,1)S(1)}, u32[]{:S(2)}, u32[]{:S(2)}) collective-permute-start(bf16[16,3200]{1,0:T(8,128)(2,1)S(1)} %pad_maximum_fusion.refs_0_), channel_id=1, source_target_pairs={{0,16},{4,20},{8,24},{12,28},{16,0},{20,4},{24,8},{28,12},{1,17},{... | collective-permute-start | bytes 307208 | tf_op jit(solution)/shard_map/ppermute | solution.py:368
  19.0 4.7 %collective-permute-start.3 = (bf16[16,3200]{1,0:T(8,128)(2,1)S(1)}, bf16[16,3200]{1,0:T(8,128)(2,1)S(1)}, u32[]{:S(2)}, u32[]{:S(2)}) collective-permute-start(bf16[16,3200]{1,0:T(8,128)(2,1)S(1)} %pad_maximum_fusion.refs_0_), channel_id=1, source_target_pairs={{0,8},{4,12},{8,0},{12,4},{16,24},{20,28},{24,16},{28,20},{1,9},{5... | collective-permute-start | bytes 307208 | tf_op jit(solution)/shard_map/ppermute | solution.py:368
  19.5 5.8 %collective-permute-start.6 = (bf16[16,3200]{1,0:T(8,128)(2,1)S(1)}, bf16[16,3200]{1,0:T(8,128)(2,1)S(1)}, u32[]{:S(2)}, u32[]{:S(2)}) collective-permute-start(bf16[16,3200]{1,0:T(8,128)(2,1)S(1)} %pad_maximum_fusion.refs_0_), channel_id=1, source_target_pairs={{0,4},{4,0},{8,12},{12,8},{1,5},{5,1},{9,13},{13,9},{2,6},{6,2},{1... | collective-permute-start | bytes 307208 | tf_op jit(solution)/shard_map/ppermute | solution.py:371
  22.3 4.2 %collective-permute-start.9 = (bf16[16,3200]{1,0:T(8,128)(2,1)S(1)}, bf16[16,3200]{1,0:T(8,128)(2,1)S(1)}, u32[]{:S(2)}, u32[]{:S(2)}) collective-permute-start(bf16[16,3200]{1,0:T(8,128)(2,1)S(1)} %collective-permute-done.5.refs_3_), channel_id=1, source_target_pairs={{0,4},{4,0},{8,12},{12,8},{1,5},{5,1},{9,13},{13,9},{2,6},{6,2},{1... | collective-permute-start | bytes 307208 | tf_op jit(solution)/shard_map/ppermute | solution.py:371
  23.3 4.2 %collective-permute-start.8 = (bf16[16,3200]{1,0:T(8,128)(2,1)S(1)}, bf16[16,3200]{1,0:T(8,128)(2,1)S(1)}, u32[]{:S(2)}, u32[]{:S(2)}) collective-permute-start(bf16[16,3200]{1,0:T(8,128)(2,1)S(1)} %collective-permute-done.4.refs_2_), channel_id=1, source_target_pairs={{0,4},{4,0},{8,12},{12,8},{1,5},{5,1},{9,13},{13,9},{2,6},{6,2},{1... | collective-permute-start | bytes 307208 | tf_op jit(solution)/shard_map/ppermute | solution.py:371
  23.6 3.8 %collective-permute-start.7 = (bf16[16,3200]{1,0:T(8,128)(2,1)S(1)}, bf16[16,3200]{1,0:T(8,128)(2,1)S(1)}, u32[]{:S(2)}, u32[]{:S(2)}) collective-permute-start(bf16[16,3200]{1,0:T(8,128)(2,1)S(1)} %collective-permute-done.3.refs_1_), channel_id=1, source_target_pairs={{0,4},{4,0},{8,12},{12,8},{1,5},{5,1},{9,13},{13,9},{2,6},{6,2},{1... | collective-permute-start | bytes 307208 | tf_op jit(solution)/shard_map/ppermute | solution.py:371
  23.9 14.8 %collective-permute-start.12 = (bf16[16,3072]{1,0:T(8,128)(2,1)S(1)}, bf16[16,3072]{1,0:T(8,128)(2,1)S(1)}, u32[]{:S(2)}, u32[]{:S(2)}) collective-permute-start(bf16[16,3072]{1,0:T(8,128)(2,1)S(1)} %pad_maximum_fusion.1.refs_0_), channel_id=1, source_target_pairs={{0,24},{4,28},{8,16},{12,20},{16,8},{20,12},{24,0},{28,4},{1,25},{... | collective-permute-start | bytes 294920 | tf_op jit(solution)/shard_map/ppermute | solution.py:368
  25.4 13.3 %collective-permute-start.11 = (bf16[16,3072]{1,0:T(8,128)(2,1)S(1)}, bf16[16,3072]{1,0:T(8,128)(2,1)S(1)}, u32[]{:S(2)}, u32[]{:S(2)}) collective-permute-start(bf16[16,3072]{1,0:T(8,128)(2,1)S(1)} %pad_maximum_fusion.1.refs_0_), channel_id=1, source_target_pairs={{0,16},{4,20},{8,24},{12,28},{16,0},{20,4},{24,8},{28,12},{1,17},{... | collective-permute-start | bytes 294920 | tf_op jit(solution)/shard_map/ppermute | solution.py:368
  26.5 12.1 %collective-permute-start.10 = (bf16[16,3072]{1,0:T(8,128)(2,1)S(1)}, bf16[16,3072]{1,0:T(8,128)(2,1)S(1)}, u32[]{:S(2)}, u32[]{:S(2)}) collective-permute-start(bf16[16,3072]{1,0:T(8,128)(2,1)S(1)} %pad_maximum_fusion.1.refs_0_), channel_id=1, source_target_pairs={{0,8},{4,12},{8,0},{12,4},{16,24},{20,28},{24,16},{28,20},{1,9},{5... | collective-permute-start | bytes 294920 | tf_op jit(solution)/shard_map/ppermute | solution.py:368
  38.6 1.4 %collective-permute-start.13 = (bf16[16,3072]{1,0:T(8,128)(2,1)S(1)}, bf16[16,3072]{1,0:T(8,128)(2,1)S(1)}, u32[]{:S(2)}, u32[]{:S(2)}) collective-permute-start(bf16[16,3072]{1,0:T(8,128)(2,1)S(1)} %pad_maximum_fusion.1.refs_0_), channel_id=1, source_target_pairs={{0,4},{4,0},{8,12},{12,8},{1,5},{5,1},{9,13},{13,9},{2,6},{6,2},{1... | collective-permute-start | bytes 294920 | tf_op jit(solution)/shard_map/ppermute | solution.py:371
  38.7 1.4 %collective-permute-start.14 = (bf16[16,3072]{1,0:T(8,128)(2,1)S(1)}, bf16[16,3072]{1,0:T(8,128)(2,1)S(1)}, u32[]{:S(2)}, u32[]{:S(2)}) collective-permute-start(bf16[16,3072]{1,0:T(8,128)(2,1)S(1)} %collective-permute-done.10.refs_1_), channel_id=1, source_target_pairs={{0,4},{4,0},{8,12},{12,8},{1,5},{5,1},{9,13},{13,9},{2,6},{6,2},{1... | collective-permute-start | bytes 294920 | tf_op jit(solution)/shard_map/ppermute | solution.py:371
  39.2 1.3 %collective-permute-start.15 = (bf16[16,3072]{1,0:T(8,128)(2,1)S(1)}, bf16[16,3072]{1,0:T(8,128)(2,1)S(1)}, u32[]{:S(2)}, u32[]{:S(2)}) collective-permute-start(bf16[16,3072]{1,0:T(8,128)(2,1)S(1)} %collective-permute-done.11.refs_2_), channel_id=1, source_target_pairs={{0,4},{4,0},{8,12},{12,8},{1,5},{5,1},{9,13},{13,9},{2,6},{6,2},{1... | collective-permute-start | bytes 294920 | tf_op jit(solution)/shard_map/ppermute | solution.py:371
  39.3 1.4 %collective-permute-start.16 = (bf16[16,3072]{1,0:T(8,128)(2,1)S(1)}, bf16[16,3072]{1,0:T(8,128)(2,1)S(1)}, u32[]{:S(2)}, u32[]{:S(2)}) collective-permute-start(bf16[16,3072]{1,0:T(8,128)(2,1)S(1)} %collective-permute-done.12.refs_3_), channel_id=1, source_target_pairs={{0,4},{4,0},{8,12},{12,8},{1,5},{5,1},{9,13},{13,9},{2,6},{6,2},{1... | collective-permute-start | bytes 294920 | tf_op jit(solution)/shard_map/ppermute | solution.py:371
  57.7 2.4 %collective-permute-start.17 = (bf16[64,6144]{1,0:T(8,128)(2,1)S(1)}, bf16[64,6144]{1,0:T(8,128)(2,1)S(1)}, u32[]{:S(2)}, u32[]{:S(2)}) collective-permute-start(bf16[64,6144]{1,0:T(8,128)(2,1)S(1)} %get-tuple-element.23), channel_id=1, source_target_pairs={{0,4},{4,0},{8,12},{12,8},{1,5},{5,1},{9,13},{13,9},{2,6},{6,2},{1... | collective-permute-start | bytes 2359304 | tf_op jit(solution)/shard_map/ppermute | solution.py:371
  60.3 7.8 %collective-permute-start.18 = (bf16[16,6144]{1,0:T(8,128)(2,1)S(1)}, bf16[16,6144]{1,0:T(8,128)(2,1)S(1)}, u32[]{:S(2)}, u32[]{:S(2)}) collective-permute-start(bf16[16,6144]{1,0:T(8,128)(2,1)S(1)} %get-tuple-element.24), channel_id=1, source_target_pairs={{0,8},{4,12},{8,0},{12,4},{16,24},{20,28},{24,16},{28,20},{1,9},{5... | collective-permute-start | bytes 589832 | tf_op jit(solution)/shard_map/ppermute | solution.py:368
  61.5 10.9 %collective-permute-start.20 = (bf16[16,6144]{1,0:T(8,128)(2,1)S(1)}, bf16[16,6144]{1,0:T(8,128)(2,1)S(1)}, u32[]{:S(2)}, u32[]{:S(2)}) collective-permute-start(bf16[16,6144]{1,0:T(8,128)(2,1)S(1)} %get-tuple-element.25), channel_id=1, source_target_pairs={{0,24},{4,28},{8,16},{12,20},{16,8},{20,12},{24,0},{28,4},{1,25},{... | collective-permute-start | bytes 589832 | tf_op jit(solution)/shard_map/ppermute | solution.py:368
  63.1 10.6 %collective-permute-start.19 = (bf16[16,6144]{1,0:T(8,128)(2,1)S(1)}, bf16[16,6144]{1,0:T(8,128)(2,1)S(1)}, u32[]{:S(2)}, u32[]{:S(2)}) collective-permute-start(bf16[16,6144]{1,0:T(8,128)(2,1)S(1)} %get-tuple-element.26), channel_id=1, source_target_pairs={{0,16},{4,20},{8,24},{12,28},{16,0},{20,4},{24,8},{28,12},{1,17},{... | collective-permute-start | bytes 589832 | tf_op jit(solution)/shard_map/ppermute | solution.py:368
  73.9 4.2 %collective-permute-start.21 = (bf16[4,6144]{1,0:T(4,128)(2,1)S(1)}, bf16[4,6144]{1,0:T(4,128)(2,1)S(1)}, u32[]{:S(2)}, u32[]{:S(2)}) collective-permute-start(bf16[4,6144]{1,0:T(4,128)(2,1)S(1)} %get-tuple-element.27), channel_id=1, source_target_pairs={{0,1},{1,0},{2,3},{3,2},{4,5},{5,4},{6,7},{7,6},{8,9},{9,8},{10,11... | collective-permute-start | bytes 147464 | tf_op jit(solution)/shard_map/ppermute | solution.py:360
  74.7 5.9 %collective-permute-start.23 = (bf16[4,6144]{1,0:T(4,128)(2,1)S(1)}, bf16[4,6144]{1,0:T(4,128)(2,1)S(1)}, u32[]{:S(2)}, u32[]{:S(2)}) collective-permute-start(bf16[4,6144]{1,0:T(4,128)(2,1)S(1)} %get-tuple-element.28), channel_id=1, source_target_pairs={{0,3},{1,2},{2,1},{3,0},{4,7},{5,6},{6,5},{7,4},{8,11},{9,10},{10,... | collective-permute-start | bytes 147464 | tf_op jit(solution)/shard_map/ppermute | solution.py:360
  77.4 5.0 %collective-permute-start.22 = (bf16[4,6144]{1,0:T(4,128)(2,1)S(1)}, bf16[4,6144]{1,0:T(4,128)(2,1)S(1)}, u32[]{:S(2)}, u32[]{:S(2)}) collective-permute-start(bf16[4,6144]{1,0:T(4,128)(2,1)S(1)} %get-tuple-element.29), channel_id=1, source_target_pairs={{0,2},{1,3},{2,0},{3,1},{4,6},{5,7},{6,4},{7,5},{8,10},{9,11},{10,... | collective-permute-start | bytes 147464 | tf_op jit(solution)/shard_map/ppermute | solution.py:360
  (8 other events, 132.2 us)

commit v3 on v2

--- a/solution.py
+++ b/solution.py
@@ -23,6 +23,11 @@
 RING = 4
 
 
+def run_of(part, depth):
+    first = depth // 8 * 3
+    return (first, depth - first) if part else (0, first)
+
+
 def three_terms(x):
     high = x.astype(BF16).astype(F32)
     mid = (x - high).astype(BF16).astype(F32)
@@ -31,8 +36,9 @@
 
 def block_copies(in_hbm, part, i, dst, sem):
     experts, depth, _, units = in_hbm.shape
-    e, s = divmod(i, depth // PARTS // STEP)
-    start = 2 * (part * (depth // PARTS) + s * STEP)
+    first, width = run_of(part, depth)
+    e, s = divmod(i, width // STEP)
+    start = 2 * (first + s * STEP)
     pairs = in_hbm.reshape(experts, 2 * depth, units)
     return [
         pltpu.make_async_copy(
@@ -137,7 +143,7 @@
     mean = jnp.sum(stream * stream, axis=1, keepdims=True) * (1.0 / width)
     normed = stream * lax.rsqrt(mean + 1e-05) * gain_ref[...].astype(F32).reshape(1, width)
     normed = normed.astype(BF16)
-    run = width // PARTS
+    run = run_of(0, width)[1]
 
     lane = lax.broadcasted_iota(jnp.int32, (reqs, LANES), 1)
     expert, field = lane % EXPERTS, lane // EXPERTS
@@ -224,14 +230,14 @@
     experts, depth, _, units = in_hbm.shape
     rows = wide.shape[0]
     slots = rows // reqs * 2
-    width = depth // PARTS
+    width = run_of(part, depth)[1]
     steps = width // STEP
     tiles = units // LANES
     from_in = {
         i: block_copies(in_hbm, part, i, ring.at[i % RING], ring_sem.at[i % RING])
         for i in range(experts * steps)
     }
-    for i in range(RING):
+    for i in range(min(RING, experts * steps)):
         for c in from_in[i]:
             c.start()
 
@@ -311,7 +317,7 @@
     n_parts = len(xs)
     rows = n_parts * xs[0].shape[0]
     slots = rows // reqs * 2
-    width = depth // PARTS
+    width = run_of(part, depth)[1]
     last = part == PARTS - 1
     half = jax.ShapeDtypeStruct((rows // 2, depth), BF16)
     acc = (experts, 2 * slots, units)
@@ -341,7 +347,7 @@
         in_specs=in_specs,
         out_specs=(VMEM,) * len(out_shape),
         scratch_shapes=scratch,
-        compiler_params=pltpu.CompilerParams(vmem_limit_bytes=(22 if last else 21) * 2**20),
+        compiler_params=pltpu.CompilerParams(vmem_limit_bytes=(23 if last else 19) * 2**20),
         cost_estimate=pl.CostEstimate(flops=10**9, bytes_accessed=100 * 10**6, transcendentals=0),
     )(*operands)
 
@@ -387,7 +393,7 @@
     )
     (expert_in,) = in_hbm(expert_in)
     column = [sent] + [turn(sent, d) for d in range(1, n_shard)]
-    cut = width // PARTS + LANES
+    cut = run_of(0, width)[1] + LANES
     columns = [jnp.concatenate(c, axis=0) for c in ([a[:, :cut] for a in column], [a[:, cut:] for a in column])]
     def aside(a):
         return [a] + [across(a, dp, dg) for dp, dg in offsets]

time: 83.3 us -> 83.4 us (level)
  transfers between devices with their start and end apart: 24 -> 24, of which waited for: 16 -> 16; matrix products, arithmetic and copies ran while one was open for 0% -> 0% of each run, Pallas kernels for 13% -> 11%
where the time goes in v3:
time: 83.4 us; the launch traced here: 83.2 us
  Pallas kernels  30.7 us (37%)
  waiting for transfers between devices  26.4 us (32%)
  starting transfers between devices  21.2 us (25%)
  local copies, waits for them, and re-layouts  2.9 us (3%)
  other arithmetic  1.13 us (1%)
  between operations  0.88 us (1%)
    pallas_call x2, Pallas kernels, experts_of(): pl.pallas_call(functools.partial(expert_kernel, part, n_parts, reqs), out...  25.6 us
    ppermute x9, waiting for transfers between devices, across(): return lax.ppermute(a, ('pool', 'grp'), pairs)  13.8 us
    ppermute x9, starting transfers between devices, across(): return lax.ppermute(a, ('pool', 'grp'), pairs)  10.7 us
    ppermute x6, starting transfers between devices, turn(): return lax.ppermute(a, 'shard', pairs)  9.31 us
    ppermute x6, waiting for transfers between devices, turn(): return lax.ppermute(a, 'shard', pairs)  9.3 us
    pallas_call x1, Pallas kernels, attend(): pl.pallas_call(attend_kernel, out_shape=(jax.ShapeDtypeStruct((reqs, widt...  5.08 us
    ppermute x9, waiting for transfers between devices, twin(): return lax.ppermute(a, 'grp', [(g, g ^ 1) for g in range(n_grp)])  3.28 us
    unnamed x16, local copies, waits for them, and re-layouts  2.71 us
  transfers between devices with their start and end apart: 24, of which 16 were waited for; matrix products, arithmetic and copies ran while one was open for 0% of the time, Pallas kernels for 11%

profile of v3, /device:TPU:0, one launch (start us, length us, event | category | flops | bytes accessed | tf_op | source)
XLA Modules:
  0.0 83.2 jit_solution(10516180933553258056)
XLA Ops:
  0.6 5.1 %shard_map.131 = (bf16[4,6144]{1,0:T(4,128)(2,1)}, bf16[4,6272]{1,0:T(4,128)(2,1)S(1)}) custom-call(s32[1,4]{1,0:T(1,128)} %table_hbm.1, s32[4]{0:T(128)} %lens_hbm.1, s32[2,4]{1,0:T(2,128)} %bitcast.5, f32[2,4]{1,0:T(2,128)} %bitcast.6, bf16[4,6144]{1,0:T(4,128)(2,1)} %q_hbm.1, bf16[4,2,1024]{2,1,0:T(2,128)(2,1)} %new_hbm.1, ...), custom_call_target="tpu_custom_call" | custom-call | flops 100000000 | bytes 20000000 | tf_op jit(solution)/shard_map/pallas_call | solution.py:174
  5.7 5.1 %collective-permute-start.2 = (bf16[4,6272]{1,0:T(4,128)(2,1)S(1)}, bf16[4,6272]{1,0:T(4,128)(2,1)S(1)}, u32[]{:S(2)}, u32[]{:S(2)}) collective-permute-start(bf16[4,6272]{1,0:T(4,128)(2,1)S(1)} %get-tuple-element.14), channel_id=1, source_target_pairs={{0,3},{1,2},{2,1},{3,0},{4,7},{5,6},{6,5},{7,4},{8,11},{9,10},{10,... | collective-permute-start | bytes 150536 | tf_op jit(solution)/shard_map/ppermute | solution.py:366
  11.5 1.6 %collective-permute-done.2 = bf16[4,6272]{1,0:T(4,128)(2,1)S(1)} collective-permute-done((bf16[4,6272]{1,0:T(4,128)(2,1)S(1)}, bf16[4,6272]{1,0:T(4,128)(2,1)S(1)}, u32[]{:S(2)}, u32[]{:S(2)}) %collective-permute-start.2) | collective-permute-done | bytes 50208 | tf_op jit(solution)/shard_map/ppermute | solution.py:366
  13.1 2.7 %collective-permute-done.1 = bf16[4,6272]{1,0:T(4,128)(2,1)S(1)} collective-permute-done((bf16[4,6272]{1,0:T(4,128)(2,1)S(1)}, bf16[4,6272]{1,0:T(4,128)(2,1)S(1)}, u32[]{:S(2)}, u32[]{:S(2)}) %collective-permute-start.1) | collective-permute-done | bytes 50208 | tf_op jit(solution)/shard_map/ppermute | solution.py:366
  15.9 2.5 %collective-permute-start.5 = (bf16[16,2432]{1,0:T(8,128)(2,1)S(1)}, bf16[16,2432]{1,0:T(8,128)(2,1)S(1)}, u32[]{:S(2)}, u32[]{:S(2)}) collective-permute-start(bf16[16,2432]{1,0:T(8,128)(2,1)S(1)} %pad_maximum_fusion.1.refs_0_), channel_id=1, source_target_pairs={{0,24},{4,28},{8,16},{12,20},{16,8},{20,12},{24,0},{28,4},{1,25},{... | collective-permute-start | bytes 233480 | tf_op jit(solution)/shard_map/ppermute | solution.py:374
  19.7 2.1 %collective-permute-done.5.refs_3_ = bf16[16,2432]{1,0:T(8,128)(2,1)S(1)} collective-permute-done((bf16[16,2432]{1,0:T(8,128)(2,1)S(1)}, bf16[16,2432]{1,0:T(8,128)(2,1)S(1)}, u32[]{:S(2)}, u32[]{:S(2)}) %collective-permute-start.5) | collective-permute-done | bytes 77856 | tf_op jit(solution)/shard_map/ppermute | solution.py:374
  21.8 1.1 %collective-permute-done.4.refs_2_ = bf16[16,2432]{1,0:T(8,128)(2,1)S(1)} collective-permute-done((bf16[16,2432]{1,0:T(8,128)(2,1)S(1)}, bf16[16,2432]{1,0:T(8,128)(2,1)S(1)}, u32[]{:S(2)}, u32[]{:S(2)}) %collective-permute-start.4) | collective-permute-done | bytes 77856 | tf_op jit(solution)/shard_map/ppermute | solution.py:374
  23.4 1.6 %collective-permute-start.12 = (bf16[16,3840]{1,0:T(8,128)(2,1)S(1)}, bf16[16,3840]{1,0:T(8,128)(2,1)S(1)}, u32[]{:S(2)}, u32[]{:S(2)}) collective-permute-start(bf16[16,3840]{1,0:T(8,128)(2,1)S(1)} %pad_maximum_fusion.refs_0_), channel_id=1, source_target_pairs={{0,24},{4,28},{8,16},{12,20},{16,8},{20,12},{24,0},{28,4},{1,25},{... | collective-permute-start | bytes 368648 | tf_op jit(solution)/shard_map/ppermute | solution.py:374
  25.0 1.0 %collective-permute-start.11 = (bf16[16,3840]{1,0:T(8,128)(2,1)S(1)}, bf16[16,3840]{1,0:T(8,128)(2,1)S(1)}, u32[]{:S(2)}, u32[]{:S(2)}) collective-permute-start(bf16[16,3840]{1,0:T(8,128)(2,1)S(1)} %pad_maximum_fusion.refs_0_), channel_id=1, source_target_pairs={{0,16},{4,20},{8,24},{12,28},{16,0},{20,4},{24,8},{28,12},{1,17},{... | collective-permute-start | bytes 368648 | tf_op jit(solution)/shard_map/ppermute | solution.py:374
  26.0 1.0 %collective-permute-start.10 = (bf16[16,3840]{1,0:T(8,128)(2,1)S(1)}, bf16[16,3840]{1,0:T(8,128)(2,1)S(1)}, u32[]{:S(2)}, u32[]{:S(2)}) collective-permute-start(bf16[16,3840]{1,0:T(8,128)(2,1)S(1)} %pad_maximum_fusion.refs_0_), channel_id=1, source_target_pairs={{0,8},{4,12},{8,0},{12,4},{16,24},{20,28},{24,16},{28,20},{1,9},{5... | collective-permute-start | bytes 368648 | tf_op jit(solution)/shard_map/ppermute | solution.py:374
  27.1 8.8 %shard_map.132 = (f32[2,128,1024]{2,1,0:T(8,128)S(1)}, f32[128,128]{1,0:T(8,128)S(1)}) custom-call(s32[1]{0:T(128)} %bitcast.2.base_ref, bf16[16,2432]{1,0:T(8,128)(2,1)S(1)} %pad_maximum_fusion.1.refs_0_, bf16[16,2432]{1,0:T(8,128)(2,1)S(1)} %collective-permute-done.3.refs_1_, bf16[16,2432]{1,0:T(8,128)(2,1)S(1)} %collective-permute-done.4.refs_2_, ...), custom_call_target="tpu_custom_call" | custom-call | flops 1000000000 | bytes 100000000 | tf_op jit(solution)/shard_map/pallas_call | solution.py:344
  38.3 1.2 %slice-done.4 = s8[4194304]{0:T(1024)(128)(4,1)S(1)} async-done(((s8[25165824]{0:T(1024)(128)(4,1)}), s8[4194304]{0:T(1024)(128)(4,1)S(1)}, s32[]{:S(2)}) %slice-start.4) | async-done | bytes 4194328
  39.5 1.2 %slice-done.5 = s8[4194304]{0:T(1024)(128)(4,1)S(1)} async-done(((s8[25165824]{0:T(1024)(128)(4,1)}), s8[4194304]{0:T(1024)(128)(4,1)S(1)}, s32[]{:S(2)}) %slice-start.5) | async-done | bytes 4194328
  40.7 16.8 %shard_map.133 = (bf16[64,6144]{1,0:T(8,128)(2,1)S(1)}, bf16[64,6144]{1,0:T(8,128)(2,1)S(1)}) custom-call(s32[1]{0:T(128)} %bitcast.2.base_ref, bf16[16,3840]{1,0:T(8,128)(2,1)S(1)} %pad_maximum_fusion.refs_0_, bf16[16,3840]{1,0:T(8,128)(2,1)S(1)} %collective-permute-done.10.refs_1_, bf16[16,3840]{1,0:T(8,128)(2,1)S(1)} %collective-permute-done.11.refs_2_, ...), custom_call_target="tpu_custom_call" | custom-call | flops 1000000000 | bytes 100000000 | tf_op jit(solution)/shard_map/pallas_call | solution.py:344
  57.6 2.3 %collective-permute-done.17 = bf16[64,6144]{1,0:T(8,128)(2,1)S(1)} collective-permute-done((bf16[64,6144]{1,0:T(8,128)(2,1)S(1)}, bf16[64,6144]{1,0:T(8,128)(2,1)S(1)}, u32[]{:S(2)}, u32[]{:S(2)}) %collective-permute-start.17) | collective-permute-done | bytes 786464 | tf_op jit(solution)/shard_map/ppermute | solution.py:377
  60.1 1.1 %collective-permute-start.18 = (bf16[16,6144]{1,0:T(8,128)(2,1)S(1)}, bf16[16,6144]{1,0:T(8,128)(2,1)S(1)}, u32[]{:S(2)}, u32[]{:S(2)}) collective-permute-start(bf16[16,6144]{1,0:T(8,128)(2,1)S(1)} %get-tuple-element.24), channel_id=1, source_target_pairs={{0,8},{4,12},{8,0},{12,4},{16,24},{20,28},{24,16},{28,20},{1,9},{5... | collective-permute-start | bytes 589832 | tf_op jit(solution)/shard_map/ppermute | solution.py:374
  61.2 1.9 %collective-permute-start.20 = (bf16[16,6144]{1,0:T(8,128)(2,1)S(1)}, bf16[16,6144]{1,0:T(8,128)(2,1)S(1)}, u32[]{:S(2)}, u32[]{:S(2)}) collective-permute-start(bf16[16,6144]{1,0:T(8,128)(2,1)S(1)} %get-tuple-element.25), channel_id=1, source_target_pairs={{0,24},{4,28},{8,16},{12,20},{16,8},{20,12},{24,0},{28,4},{1,25},{... | collective-permute-start | bytes 589832 | tf_op jit(solution)/shard_map/ppermute | solution.py:374
  63.7 4.3 %collective-permute-done.18 = bf16[16,6144]{1,0:T(8,128)(2,1)S(1)} collective-permute-done((bf16[16,6144]{1,0:T(8,128)(2,1)S(1)}, bf16[16,6144]{1,0:T(8,128)(2,1)S(1)}, u32[]{:S(2)}, u32[]{:S(2)}) %collective-permute-start.18) | collective-permute-done | bytes 196640 | tf_op jit(solution)/shard_map/ppermute | solution.py:374
  67.9 4.5 %collective-permute-done.20 = bf16[16,6144]{1,0:T(8,128)(2,1)S(1)} collective-permute-done((bf16[16,6144]{1,0:T(8,128)(2,1)S(1)}, bf16[16,6144]{1,0:T(8,128)(2,1)S(1)}, u32[]{:S(2)}, u32[]{:S(2)}) %collective-permute-start.20) | collective-permute-done | bytes 196640 | tf_op jit(solution)/shard_map/ppermute | solution.py:374
  72.4 1.4 %collective-permute-done.19 = bf16[16,6144]{1,0:T(8,128)(2,1)S(1)} collective-permute-done((bf16[16,6144]{1,0:T(8,128)(2,1)S(1)}, bf16[16,6144]{1,0:T(8,128)(2,1)S(1)}, u32[]{:S(2)}, u32[]{:S(2)}) %collective-permute-start.19) | collective-permute-done | bytes 196640 | tf_op jit(solution)/shard_map/ppermute | solution.py:374
  74.0 0.7 collective-permute-start.21
  74.7 2.8 %collective-permute-start.23 = (bf16[4,6144]{1,0:T(4,128)(2,1)S(1)}, bf16[4,6144]{1,0:T(4,128)(2,1)S(1)}, u32[]{:S(2)}, u32[]{:S(2)}) collective-permute-start(bf16[4,6144]{1,0:T(4,128)(2,1)S(1)} %get-tuple-element.28), channel_id=1, source_target_pairs={{0,3},{1,2},{2,1},{3,0},{4,7},{5,6},{6,5},{7,4},{8,11},{9,10},{10,... | collective-permute-start | bytes 147464 | tf_op jit(solution)/shard_map/ppermute | solution.py:366
  78.1 2.5 %collective-permute-done.23 = bf16[4,6144]{1,0:T(4,128)(2,1)S(1)} collective-permute-done((bf16[4,6144]{1,0:T(4,128)(2,1)S(1)}, bf16[4,6144]{1,0:T(4,128)(2,1)S(1)}, u32[]{:S(2)}, u32[]{:S(2)}) %collective-permute-start.23) | collective-permute-done | bytes 49184 | tf_op jit(solution)/shard_map/ppermute | solution.py:366
  80.6 1.9 %collective-permute-done.22 = bf16[4,6144]{1,0:T(4,128)(2,1)S(1)} collective-permute-done((bf16[4,6144]{1,0:T(4,128)(2,1)S(1)}, bf16[4,6144]{1,0:T(4,128)(2,1)S(1)}, u32[]{:S(2)}, u32[]{:S(2)}) %collective-permute-start.22) | collective-permute-done | bytes 49184 | tf_op jit(solution)/shard_map/ppermute | solution.py:366
  (59 shorter events, 7.2 us)
Async XLA Ops:
  5.7 7.4 %collective-permute-start.2 = (bf16[4,6272]{1,0:T(4,128)(2,1)S(1)}, bf16[4,6272]{1,0:T(4,128)(2,1)S(1)}, u32[]{:S(2)}, u32[]{:S(2)}) collective-permute-start(bf16[4,6272]{1,0:T(4,128)(2,1)S(1)} %get-tuple-element.14), channel_id=1, source_target_pairs={{0,3},{1,2},{2,1},{3,0},{4,7},{5,6},{6,5},{7,4},{8,11},{9,10},{10,... | collective-permute-start | bytes 150536 | tf_op jit(solution)/shard_map/ppermute | solution.py:366
  10.8 5.0 %collective-permute-start.1 = (bf16[4,6272]{1,0:T(4,128)(2,1)S(1)}, bf16[4,6272]{1,0:T(4,128)(2,1)S(1)}, u32[]{:S(2)}, u32[]{:S(2)}) collective-permute-start(bf16[4,6272]{1,0:T(4,128)(2,1)S(1)} %get-tuple-element.14), channel_id=1, source_target_pairs={{0,2},{1,3},{2,0},{3,1},{4,6},{5,7},{6,4},{7,5},{8,10},{9,11},{10,... | collective-permute-start | bytes 150536 | tf_op jit(solution)/shard_map/ppermute | solution.py:366
  10.8 5.0 %collective-permute-start = (bf16[4,6272]{1,0:T(4,128)(2,1)S(1)}, bf16[4,6272]{1,0:T(4,128)(2,1)S(1)}, u32[]{:S(2)}, u32[]{:S(2)}) collective-permute-start(bf16[4,6272]{1,0:T(4,128)(2,1)S(1)} %get-tuple-element.14), channel_id=1, source_target_pairs={{0,1},{1,0},{2,3},{3,2},{4,5},{5,4},{6,7},{7,6},{8,9},{9,8},{10,11... | collective-permute-start | bytes 150536 | tf_op jit(solution)/shard_map/ppermute | solution.py:366
  15.9 5.8 %collective-permute-start.5 = (bf16[16,2432]{1,0:T(8,128)(2,1)S(1)}, bf16[16,2432]{1,0:T(8,128)(2,1)S(1)}, u32[]{:S(2)}, u32[]{:S(2)}) collective-permute-start(bf16[16,2432]{1,0:T(8,128)(2,1)S(1)} %pad_maximum_fusion.1.refs_0_), channel_id=1, source_target_pairs={{0,24},{4,28},{8,16},{12,20},{16,8},{20,12},{24,0},{28,4},{1,25},{... | collective-permute-start | bytes 233480 | tf_op jit(solution)/shard_map/ppermute | solution.py:374
  18.5 4.4 %collective-permute-start.4 = (bf16[16,2432]{1,0:T(8,128)(2,1)S(1)}, bf16[16,2432]{1,0:T(8,128)(2,1)S(1)}, u32[]{:S(2)}, u32[]{:S(2)}) collective-permute-start(bf16[16,2432]{1,0:T(8,128)(2,1)S(1)} %pad_maximum_fusion.1.refs_0_), channel_id=1, source_target_pairs={{0,16},{4,20},{8,24},{12,28},{16,0},{20,4},{24,8},{28,12},{1,17},{... | collective-permute-start | bytes 233480 | tf_op jit(solution)/shard_map/ppermute | solution.py:374
  19.0 4.4 %collective-permute-start.3 = (bf16[16,2432]{1,0:T(8,128)(2,1)S(1)}, bf16[16,2432]{1,0:T(8,128)(2,1)S(1)}, u32[]{:S(2)}, u32[]{:S(2)}) collective-permute-start(bf16[16,2432]{1,0:T(8,128)(2,1)S(1)} %pad_maximum_fusion.1.refs_0_), channel_id=1, source_target_pairs={{0,8},{4,12},{8,0},{12,4},{16,24},{20,28},{24,16},{28,20},{1,9},{5... | collective-permute-start | bytes 233480 | tf_op jit(solution)/shard_map/ppermute | solution.py:374
  19.5 5.5 %collective-permute-start.6 = (bf16[16,2432]{1,0:T(8,128)(2,1)S(1)}, bf16[16,2432]{1,0:T(8,128)(2,1)S(1)}, u32[]{:S(2)}, u32[]{:S(2)}) collective-permute-start(bf16[16,2432]{1,0:T(8,128)(2,1)S(1)} %pad_maximum_fusion.1.refs_0_), channel_id=1, source_target_pairs={{0,4},{4,0},{8,12},{12,8},{1,5},{5,1},{9,13},{13,9},{2,6},{6,2},{1... | collective-permute-start | bytes 233480 | tf_op jit(solution)/shard_map/ppermute | solution.py:377
  21.8 4.2 %collective-permute-start.9 = (bf16[16,2432]{1,0:T(8,128)(2,1)S(1)}, bf16[16,2432]{1,0:T(8,128)(2,1)S(1)}, u32[]{:S(2)}, u32[]{:S(2)}) collective-permute-start(bf16[16,2432]{1,0:T(8,128)(2,1)S(1)} %collective-permute-done.5.refs_3_), channel_id=1, source_target_pairs={{0,4},{4,0},{8,12},{12,8},{1,5},{5,1},{9,13},{13,9},{2,6},{6,2},{1... | collective-permute-start | bytes 233480 | tf_op jit(solution)/shard_map/ppermute | solution.py:377
  22.8 4.2 %collective-permute-start.8 = (bf16[16,2432]{1,0:T(8,128)(2,1)S(1)}, bf16[16,2432]{1,0:T(8,128)(2,1)S(1)}, u32[]{:S(2)}, u32[]{:S(2)}) collective-permute-start(bf16[16,2432]{1,0:T(8,128)(2,1)S(1)} %collective-permute-done.4.refs_2_), channel_id=1, source_target_pairs={{0,4},{4,0},{8,12},{12,8},{1,5},{5,1},{9,13},{13,9},{2,6},{6,2},{1... | collective-permute-start | bytes 233480 | tf_op jit(solution)/shard_map/ppermute | solution.py:377
  23.4 3.7 %collective-permute-start.7 = (bf16[16,2432]{1,0:T(8,128)(2,1)S(1)}, bf16[16,2432]{1,0:T(8,128)(2,1)S(1)}, u32[]{:S(2)}, u32[]{:S(2)}) collective-permute-start(bf16[16,2432]{1,0:T(8,128)(2,1)S(1)} %collective-permute-done.3.refs_1_), channel_id=1, source_target_pairs={{0,4},{4,0},{8,12},{12,8},{1,5},{5,1},{9,13},{13,9},{2,6},{6,2},{1... | collective-permute-start | bytes 233480 | tf_op jit(solution)/shard_map/ppermute | solution.py:377
  23.4 12.5 %collective-permute-start.12 = (bf16[16,3840]{1,0:T(8,128)(2,1)S(1)}, bf16[16,3840]{1,0:T(8,128)(2,1)S(1)}, u32[]{:S(2)}, u32[]{:S(2)}) collective-permute-start(bf16[16,3840]{1,0:T(8,128)(2,1)S(1)} %pad_maximum_fusion.refs_0_), channel_id=1, source_target_pairs={{0,24},{4,28},{8,16},{12,20},{16,8},{20,12},{24,0},{28,4},{1,25},{... | collective-permute-start | bytes 368648 | tf_op jit(solution)/shard_map/ppermute | solution.py:374
  25.0 10.9 %collective-permute-start.11 = (bf16[16,3840]{1,0:T(8,128)(2,1)S(1)}, bf16[16,3840]{1,0:T(8,128)(2,1)S(1)}, u32[]{:S(2)}, u32[]{:S(2)}) collective-permute-start(bf16[16,3840]{1,0:T(8,128)(2,1)S(1)} %pad_maximum_fusion.refs_0_), channel_id=1, source_target_pairs={{0,16},{4,20},{8,24},{12,28},{16,0},{20,4},{24,8},{28,12},{1,17},{... | collective-permute-start | bytes 368648 | tf_op jit(solution)/shard_map/ppermute | solution.py:374
  26.0 9.9 %collective-permute-start.10 = (bf16[16,3840]{1,0:T(8,128)(2,1)S(1)}, bf16[16,3840]{1,0:T(8,128)(2,1)S(1)}, u32[]{:S(2)}, u32[]{:S(2)}) collective-permute-start(bf16[16,3840]{1,0:T(8,128)(2,1)S(1)} %pad_maximum_fusion.refs_0_), channel_id=1, source_target_pairs={{0,8},{4,12},{8,0},{12,4},{16,24},{20,28},{24,16},{28,20},{1,9},{5... | collective-permute-start | bytes 368648 | tf_op jit(solution)/shard_map/ppermute | solution.py:374
  35.9 1.4 %collective-permute-start.13 = (bf16[16,3840]{1,0:T(8,128)(2,1)S(1)}, bf16[16,3840]{1,0:T(8,128)(2,1)S(1)}, u32[]{:S(2)}, u32[]{:S(2)}) collective-permute-start(bf16[16,3840]{1,0:T(8,128)(2,1)S(1)} %pad_maximum_fusion.refs_0_), channel_id=1, source_target_pairs={{0,4},{4,0},{8,12},{12,8},{1,5},{5,1},{9,13},{13,9},{2,6},{6,2},{1... | collective-permute-start | bytes 368648 | tf_op jit(solution)/shard_map/ppermute | solution.py:377
  36.0 1.5 %collective-permute-start.14 = (bf16[16,3840]{1,0:T(8,128)(2,1)S(1)}, bf16[16,3840]{1,0:T(8,128)(2,1)S(1)}, u32[]{:S(2)}, u32[]{:S(2)}) collective-permute-start(bf16[16,3840]{1,0:T(8,128)(2,1)S(1)} %collective-permute-done.10.refs_1_), channel_id=1, source_target_pairs={{0,4},{4,0},{8,12},{12,8},{1,5},{5,1},{9,13},{13,9},{2,6},{6,2},{1... | collective-permute-start | bytes 368648 | tf_op jit(solution)/shard_map/ppermute | solution.py:377
  36.5 1.3 %collective-permute-start.15 = (bf16[16,3840]{1,0:T(8,128)(2,1)S(1)}, bf16[16,3840]{1,0:T(8,128)(2,1)S(1)}, u32[]{:S(2)}, u32[]{:S(2)}) collective-permute-start(bf16[16,3840]{1,0:T(8,128)(2,1)S(1)} %collective-permute-done.11.refs_2_), channel_id=1, source_target_pairs={{0,4},{4,0},{8,12},{12,8},{1,5},{5,1},{9,13},{13,9},{2,6},{6,2},{1... | collective-permute-start | bytes 368648 | tf_op jit(solution)/shard_map/ppermute | solution.py:377
  36.6 1.4 %collective-permute-start.16 = (bf16[16,3840]{1,0:T(8,128)(2,1)S(1)}, bf16[16,3840]{1,0:T(8,128)(2,1)S(1)}, u32[]{:S(2)}, u32[]{:S(2)}) collective-permute-start(bf16[16,3840]{1,0:T(8,128)(2,1)S(1)} %collective-permute-done.12.refs_3_), channel_id=1, source_target_pairs={{0,4},{4,0},{8,12},{12,8},{1,5},{5,1},{9,13},{13,9},{2,6},{6,2},{1... | collective-permute-start | bytes 368648 | tf_op jit(solution)/shard_map/ppermute | solution.py:377
  57.5 2.4 %collective-permute-start.17 = (bf16[64,6144]{1,0:T(8,128)(2,1)S(1)}, bf16[64,6144]{1,0:T(8,128)(2,1)S(1)}, u32[]{:S(2)}, u32[]{:S(2)}) collective-permute-start(bf16[64,6144]{1,0:T(8,128)(2,1)S(1)} %get-tuple-element.23), channel_id=1, source_target_pairs={{0,4},{4,0},{8,12},{12,8},{1,5},{5,1},{9,13},{13,9},{2,6},{6,2},{1... | collective-permute-start | bytes 2359304 | tf_op jit(solution)/shard_map/ppermute | solution.py:377
  60.1 7.8 %collective-permute-start.18 = (bf16[16,6144]{1,0:T(8,128)(2,1)S(1)}, bf16[16,6144]{1,0:T(8,128)(2,1)S(1)}, u32[]{:S(2)}, u32[]{:S(2)}) collective-permute-start(bf16[16,6144]{1,0:T(8,128)(2,1)S(1)} %get-tuple-element.24), channel_id=1, source_target_pairs={{0,8},{4,12},{8,0},{12,4},{16,24},{20,28},{24,16},{28,20},{1,9},{5... | collective-permute-start | bytes 589832 | tf_op jit(solution)/shard_map/ppermute | solution.py:374
  61.2 11.2 %collective-permute-start.20 = (bf16[16,6144]{1,0:T(8,128)(2,1)S(1)}, bf16[16,6144]{1,0:T(8,128)(2,1)S(1)}, u32[]{:S(2)}, u32[]{:S(2)}) collective-permute-start(bf16[16,6144]{1,0:T(8,128)(2,1)S(1)} %get-tuple-element.25), channel_id=1, source_target_pairs={{0,24},{4,28},{8,16},{12,20},{16,8},{20,12},{24,0},{28,4},{1,25},{... | collective-permute-start | bytes 589832 | tf_op jit(solution)/shard_map/ppermute | solution.py:374
  63.2 10.6 %collective-permute-start.19 = (bf16[16,6144]{1,0:T(8,128)(2,1)S(1)}, bf16[16,6144]{1,0:T(8,128)(2,1)S(1)}, u32[]{:S(2)}, u32[]{:S(2)}) collective-permute-start(bf16[16,6144]{1,0:T(8,128)(2,1)S(1)} %get-tuple-element.26), channel_id=1, source_target_pairs={{0,16},{4,20},{8,24},{12,28},{16,0},{20,4},{24,8},{28,12},{1,17},{... | collective-permute-start | bytes 589832 | tf_op jit(solution)/shard_map/ppermute | solution.py:374
  74.0 4.2 %collective-permute-start.21 = (bf16[4,6144]{1,0:T(4,128)(2,1)S(1)}, bf16[4,6144]{1,0:T(4,128)(2,1)S(1)}, u32[]{:S(2)}, u32[]{:S(2)}) collective-permute-start(bf16[4,6144]{1,0:T(4,128)(2,1)S(1)} %get-tuple-element.27), channel_id=1, source_target_pairs={{0,1},{1,0},{2,3},{3,2},{4,5},{5,4},{6,7},{7,6},{8,9},{9,8},{10,11... | collective-permute-start | bytes 147464 | tf_op jit(solution)/shard_map/ppermute | solution.py:366
  74.7 5.9 %collective-permute-start.23 = (bf16[4,6144]{1,0:T(4,128)(2,1)S(1)}, bf16[4,6144]{1,0:T(4,128)(2,1)S(1)}, u32[]{:S(2)}, u32[]{:S(2)}) collective-permute-start(bf16[4,6144]{1,0:T(4,128)(2,1)S(1)} %get-tuple-element.28), channel_id=1, source_target_pairs={{0,3},{1,2},{2,1},{3,0},{4,7},{5,6},{6,5},{7,4},{8,11},{9,10},{10,... | collective-permute-start | bytes 147464 | tf_op jit(solution)/shard_map/ppermute | solution.py:366
  77.5 5.0 %collective-permute-start.22 = (bf16[4,6144]{1,0:T(4,128)(2,1)S(1)}, bf16[4,6144]{1,0:T(4,128)(2,1)S(1)}, u32[]{:S(2)}, u32[]{:S(2)}) collective-permute-start(bf16[4,6144]{1,0:T(4,128)(2,1)S(1)} %get-tuple-element.29), channel_id=1, source_target_pairs={{0,2},{1,3},{2,0},{3,1},{4,6},{5,7},{6,4},{7,5},{8,10},{9,11},{10,... | collective-permute-start | bytes 147464 | tf_op jit(solution)/shard_map/ppermute | solution.py:366
  (8 other events, 120.3 us)
